TPU v7x, 256 devices: a whole 4x4x8 slice. The times are simulated.
256 devices in a mesh: trainer: 64 (over z, x, core), mp: 4 (over y).
Axes of the slice: x: 4, y: 4, z: 8, core: 2. Of those that a mesh axis runs over, the one named last changes fastest.
Arguments:
- history: bfloat16 [3, 131072, 1024], P(None, 'trainer', 'mp'), may hold values from -6 to 6
- send_rows: int32 [64, 64, 48], P('trainer'), may hold values from 0 to 2047
- batch_ids: int32 [64, 1024], P('trainer'), may hold values from 0 to 2047, as said below
- block_cols: int32 [512, 12], P('trainer'), may hold values from 0 to 31, as said below
- block_count: int32 [512], P('trainer'), may hold values from 1 to 12, as said below
- adjacency: bfloat16 [512, 12, 128, 128], P('trainer'), may hold values from -0.15625 to 0.15625
- weights: bfloat16 [3, 1024, 1024], P(None, None, 'mp'), may hold values from -0.1875 to 0.1875
- cotangent: bfloat16 [65536, 1024], P('trainer', 'mp'), may hold values from -0.0234375 to 0.0234375
Outputs:
- fresh_history: bfloat16 [2, 131072, 1024], P(None, 'trainer', 'mp')
- final_output: bfloat16 [65536, 1024], P('trainer', 'mp')
- weight_grad: float32 [1024, 1024], P('trainer', 'mp')
Inputs may be any that keep to these rules, and one draw needn't show every extreme that they name: `send_rows`: rows of the sending owner's own history. `batch_ids`: the 1024 entries of one trainer are distinct; at most half of a trainer's history rows are in its batch. `block_cols`: the 12 slots of one row block name distinct column blocks; blocks below 8 are batch rows, the rest halo rows. `block_count`: slots from the count on are ignored; in every draw some trainers have all row blocks at 12.
All inputs are finite; a program needn't handle non-finite values.
Results may differ from a plain program's by a relative error of at most 0.0054.
Values may be sent and summed in bfloat16 or wider, within the bound.
No kernel may reach another device: no remote copies, remote signals or barrier semaphores. Data moves between devices by JAX's collectives and lax.ppermute only.
A program may use at most 64 MiB of HBM per device.

v0:
```python
import math

import jax
import jax.numpy as jnp
from jax import lax
from jax.sharding import PartitionSpec as P

LAYERS = 3


mixing = 0.1
strength = 0.5


def layer_share(layer_index):
    return math.log(strength / (layer_index + 1) + 1.0)


def aggregate_blocks(stacked, column_ids, counts, blocks_here):
    feature_width = stacked.shape[1]
    block_side = blocks_here.shape[2]
    blocks = stacked.reshape(-1, block_side, feature_width)
    picked = blocks[column_ids]
    active = jnp.arange(column_ids.shape[1], dtype=jnp.int32)[None, :] < counts[:, None]
    masked = jnp.where(active[:, :, None, None], blocks_here, jnp.zeros_like(blocks_here))
    summed = jnp.einsum("rkij,rkjd->rid", masked, picked, preferred_element_type=jnp.float32)
    return summed.reshape(-1, feature_width)


def fold_columns(support, weight, cotangent, final_layer):

    def add_columns(column_block):
        updated = jnp.dot(column_block, weight, preferred_element_type=jnp.float32)
        if final_layer:
            partial_grad = lax.dot_general(
                column_block,
                cotangent,
                (((0,), (0,)), ((), ())),
                preferred_element_type=jnp.float32,
            )
            return (updated, partial_grad)
        return (updated,)

    return add_columns(lax.all_gather(support, "mp", axis=1, tiled=True))


def body(history, send_rows, batch_ids, block_cols, block_count, adjacency, weights, cotangent):
    feature_width = history.shape[2]
    local_ids = batch_ids[0]
    start_rows = history[0][local_ids]
    current = start_rows
    fresh_rows = []
    for layer_index in range(LAYERS):
        halo_rows = lax.all_to_all(
            history[layer_index][send_rows[0]], "trainer", split_axis=0, concat_axis=0, tiled=True
        ).reshape(-1, feature_width)
        stacked = jnp.concatenate([current, halo_rows], 0)
        aggregate = aggregate_blocks(stacked, block_cols, block_count, adjacency)
        support = ((1.0 - mixing) * aggregate + mixing * start_rows.astype(jnp.float32)).astype(
            jnp.bfloat16
        )
        share = layer_share(layer_index)
        final_layer = layer_index + 1 == LAYERS
        totals = fold_columns(support, weights[layer_index], cotangent, final_layer)
        mixed = (1.0 - share) * support.astype(jnp.float32) + share * totals[0]
        if not final_layer:
            current = jax.nn.relu(mixed).astype(jnp.bfloat16)
            fresh_rows.append(history[layer_index + 1].at[local_ids].set(current))
    grad_rows = lax.psum_scatter(
        totals[1], "trainer", scatter_dimension=0, tiled=True
    ) * layer_share(LAYERS - 1)
    return (jnp.stack(fresh_rows), mixed.astype(jnp.bfloat16), grad_rows)


def solution(mesh):
    return jax.shard_map(
        body,
        mesh=mesh,
        in_specs=(
            P(None, "trainer", "mp"),
            P("trainer", None, None),
            P("trainer", None),
            P("trainer", None),
            P("trainer"),
            P("trainer", None, None, None),
            P(None, None, "mp"),
            P("trainer", "mp"),
        ),
        out_specs=(P(None, "trainer", "mp"), P("trainer", "mp"), P("trainer", "mp")),
        check_vma=False,
    )
```

profile of v0, /device:TPU:8, one launch (start us, length us, event | category | flops | bytes accessed | tf_op | source)
XLA Modules:
  0.0 428.1 jit_solution(16002498190228371548)
XLA Ops:
  10.5 13.6 %gather_fusion.1 = bf16[3072,256]{1,0:T(8,128)(2,1)} fusion(bf16[2048,256]{1,0:T(8,128)(2,1)} %get-tuple-element.3, s32[3072]{0:T(1024)S(1)} %broadcast_clamp_fusion), kind=kCustom, calls=%fused_computation.1 | custom fusion | bytes 3158016 | tf_op jit(solution)/shard_map/gather | solution.py:55
  24.1 12.3 %all-to-all-start = ((bf16[64,48,256]{2,1,0:T(8,128)(2,1)}), bf16[64,48,256]{2,1,0:T(8,128)(2,1)}, u32[]{:S(2)}, u32[]{:S(2)}) async-start(bf16[64,48,256]{2,1,0:T(8,128)(2,1)} %bitcast.79), calls=%async_computation | async-start | bytes 3145728 | tf_op jit(solution)/shard_map/all_to_all | solution.py:54
  36.5 4.8 %gather_fusion = bf16[1024,256]{1,0:T(8,128)(2,1)S(1)} fusion(bf16[2048,256]{1,0:T(8,128)(2,1)} %get-tuple-element.3, s32[1024]{0:T(1024)S(1)} %broadcast_clamp_fusion.1), kind=kCustom, calls=%fused_computation | custom fusion | bytes 1052672 | tf_op jit(solution)/shard_map/gather | solution.py:50
  41.5 34.9 %all-to-all-done = bf16[64,48,256]{2,1,0:T(8,128)(2,1)} async-done(((bf16[64,48,256]{2,1,0:T(8,128)(2,1)}), bf16[64,48,256]{2,1,0:T(8,128)(2,1)}, u32[]{:S(2)}, u32[]{:S(2)}) %all-to-all-start) | async-done | bytes 1572896 | tf_op jit(solution)/shard_map/all_to_all | solution.py:54
  79.2 7.6 %gather_fusion.2 = bf16[96,128,256]{2,1,0:T(8,128)(2,1)} fusion(bf16[32,128,256]{2,1,0:T(8,128)(2,1)} %bitcast.74, s32[1024]{0:T(1024)S(1)} %pad_clamp_fusion), kind=kCustom, calls=%fused_computation.2 | custom fusion | bytes 12583296 | tf_op jit(solution)/shard_map/gather | solution.py:23
  86.8 4.8 %fusion.16 = f32[8,128,256]{2,1,0:T(8,128)S(1)} fusion(bf16[8,12,128,256]{3,2,1,0:T(8,128)(2,1)} %bitcast.77, bf16[8,12,128,128]{3,2,1,0:T(8,128)(2,1)} %param.13, pred[8,12]{1,0:T(8,128)(4,1)S(1)} %iota_compare_fusion), kind=kOutput, calls=%fused_computation.33 | convolution fusion | flops 807141376 | bytes 10485856 | tf_op jit(solution)/shard_map/rkij,rkjd->rid/dot_general | solution.py:26
  92.6 13.0 %gather_fusion.3 = bf16[3072,256]{1,0:T(8,128)(2,1)} fusion(bf16[2048,256]{1,0:T(8,128)(2,1)S(1)} %get-tuple-element.4, s32[3072]{0:T(1024)S(1)} %broadcast_clamp_fusion), kind=kCustom, calls=%fused_computation.3 | custom fusion | bytes 3158016 | tf_op jit(solution)/shard_map/gather | solution.py:55
  105.6 5.6 %all-to-all-start.1 = ((bf16[64,48,256]{2,1,0:T(8,128)(2,1)}), bf16[64,48,256]{2,1,0:T(8,128)(2,1)}, u32[]{:S(2)}, u32[]{:S(2)}) async-start(bf16[64,48,256]{2,1,0:T(8,128)(2,1)} %bitcast.81), calls=%async_computation.1 | async-start | bytes 3145728 | tf_op jit(solution)/shard_map/all_to_all | solution.py:54
  111.3 14.1 %all-gather.4.cloned.1.call-done = bf16[1024,1024]{1,0:T(8,128)(2,1)} async-done(((bf16[1024,256]{1,0:T(8,128)(2,1)}), bf16[1024,1024]{1,0:T(8,128)(2,1)}) %all-gather.4.cloned.1.call-update) | async-done | bytes 2097168 | tf_op jit(solution)/shard_map/all_gather | solution.py:44
  125.4 3.3 fusion.18
  128.7 22.5 %all-to-all-done.1 = bf16[64,48,256]{2,1,0:T(8,128)(2,1)} async-done(((bf16[64,48,256]{2,1,0:T(8,128)(2,1)}), bf16[64,48,256]{2,1,0:T(8,128)(2,1)}, u32[]{:S(2)}, u32[]{:S(2)}) %all-to-all-start.1) | async-done | bytes 1572896 | tf_op jit(solution)/shard_map/all_to_all | solution.py:54
  154.2 7.6 %gather_fusion.4 = bf16[96,128,256]{2,1,0:T(8,128)(2,1)} fusion(bf16[32,128,256]{2,1,0:T(8,128)(2,1)} %bitcast.75, s32[1024]{0:T(1024)S(1)} %pad_clamp_fusion), kind=kCustom, calls=%fused_computation.4 | custom fusion | bytes 12583296 | tf_op jit(solution)/shard_map/gather | solution.py:23
  161.8 4.8 %fusion.15 = f32[8,128,256]{2,1,0:T(8,128)S(1)} fusion(bf16[8,12,128,256]{3,2,1,0:T(8,128)(2,1)} %bitcast.78, bf16[8,12,128,128]{3,2,1,0:T(8,128)(2,1)} %param.13, pred[8,12]{1,0:T(8,128)(4,1)S(1)} %iota_compare_fusion), kind=kOutput, calls=%fused_computation.32 | convolution fusion | flops 807141376 | bytes 10485856 | tf_op jit(solution)/shard_map/rkij,rkjd->rid/dot_general | solution.py:26
  167.5 13.0 %gather_fusion.5 = bf16[3072,256]{1,0:T(8,128)(2,1)} fusion(bf16[2048,256]{1,0:T(8,128)(2,1)S(1)} %get-tuple-element.5, s32[3072]{0:T(1024)S(1)} %broadcast_clamp_fusion), kind=kCustom, calls=%fused_computation.5 | custom fusion | bytes 3158016 | tf_op jit(solution)/shard_map/gather | solution.py:55
  180.6 5.6 %all-to-all-start.2 = ((bf16[64,48,256]{2,1,0:T(8,128)(2,1)}), bf16[64,48,256]{2,1,0:T(8,128)(2,1)}, u32[]{:S(2)}, u32[]{:S(2)}) async-start(bf16[64,48,256]{2,1,0:T(8,128)(2,1)} %bitcast.80), calls=%async_computation.2 | async-start | bytes 3145728 | tf_op jit(solution)/shard_map/all_to_all | solution.py:54
  186.4 13.9 %all-gather.6.cloned.1.call-done = bf16[1024,1024]{1,0:T(8,128)(2,1)} async-done(((bf16[1024,256]{1,0:T(8,128)(2,1)}), bf16[1024,1024]{1,0:T(8,128)(2,1)}) %all-gather.6.cloned.1.call-update) | async-done | bytes 2097168 | tf_op jit(solution)/shard_map/all_gather | solution.py:44
  200.3 3.3 fusion.19
  203.7 22.5 %all-to-all-done.2 = bf16[64,48,256]{2,1,0:T(8,128)(2,1)} async-done(((bf16[64,48,256]{2,1,0:T(8,128)(2,1)}), bf16[64,48,256]{2,1,0:T(8,128)(2,1)}, u32[]{:S(2)}, u32[]{:S(2)}) %all-to-all-start.2) | async-done | bytes 1572896 | tf_op jit(solution)/shard_map/all_to_all | solution.py:54
  229.1 7.6 %gather_fusion.6 = bf16[96,128,256]{2,1,0:T(8,128)(2,1)} fusion(bf16[32,128,256]{2,1,0:T(8,128)(2,1)} %bitcast.73, s32[1024]{0:T(1024)S(1)} %pad_clamp_fusion), kind=kCustom, calls=%fused_computation.6 | custom fusion | bytes 12583296 | tf_op jit(solution)/shard_map/gather | solution.py:23
  236.7 4.8 %fusion.14 = f32[8,128,256]{2,1,0:T(8,128)S(1)} fusion(bf16[8,12,128,256]{3,2,1,0:T(8,128)(2,1)} %bitcast.76, bf16[8,12,128,128]{3,2,1,0:T(8,128)(2,1)} %param.13, pred[8,12]{1,0:T(8,128)(4,1)S(1)} %iota_compare_fusion), kind=kOutput, calls=%fused_computation.31 | convolution fusion | flops 807141376 | bytes 10485856 | tf_op jit(solution)/shard_map/rkij,rkjd->rid/dot_general | solution.py:26
  242.6 32.8 %all-gather.8.cloned.1.call-done = bf16[1024,1024]{1,0:T(8,128)(2,1)} async-done(((bf16[1024,256]{1,0:T(8,128)(2,1)}), bf16[1024,1024]{1,0:T(8,128)(2,1)}) %all-gather.8.cloned.1.call-update) | async-done | bytes 2097168 | tf_op jit(solution)/shard_map/all_gather | solution.py:44
  278.7 5.5 %scatter_fusion = bf16[2048,256]{1,0:T(8,128)(2,1)S(1)} fusion(bf16[2048,256]{1,0:T(8,128)(2,1)S(1)} %get-tuple-element.4, s32[1024]{0:T(1024)S(1)} %bitcast.83, bf16[1024,256]{1,0:T(8,128)(2,1)S(1)} %copy-done.2), kind=kCustom, calls=%fused_computation.7 | custom fusion | bytes 1576960 | tf_op jit(solution)/shard_map/scatter | solution.py:68
  284.2 5.9 %scatter_fusion.1 = bf16[2048,256]{1,0:T(8,128)(2,1)S(1)} fusion(bf16[2048,256]{1,0:T(8,128)(2,1)S(1)} %get-tuple-element.5, s32[1024]{0:T(1024)S(1)} %bitcast.84, bf16[1024,256]{1,0:T(8,128)(2,1)} %fusion.19), kind=kCustom, calls=%fused_computation.8 | custom fusion | bytes 1576960 | tf_op jit(solution)/shard_map/scatter | solution.py:68
  295.2 125.1 %reduce-scatter.2.cloned.1.call-done = f32[16,256]{1,0:T(8,128)} async-done(((f32[1024,256]{1,0:T(8,128)}), f32[16,256]{1,0:T(8,128)}) %reduce-scatter.2.cloned.1.call-update) | async-done | bytes 16400 | tf_op jit(solution)/shard_map/reduce_scatter | solution.py:69
  (45 shorter events, 25.2 us)
Async XLA Ops:
  7.2 268.1 %copy-start = (bf16[1024,256]{1,0:T(8,128)(2,1)S(1)}, bf16[1024,256]{1,0:T(8,128)(2,1)}, u32[]{:S(2)}) copy-start(bf16[1024,256]{1,0:T(8,128)(2,1)} %param.15) | copy-start | bytes 1572868
  7.2 3.1 copy-start.3
  24.1 12.4 %copy-start.4 = (s32[1,1024]{1,0:T(1,128)S(1)}, s32[1,1024]{1,0:T(1,128)}, u32[]{:S(2)}) copy-start(s32[1,1024]{1,0:T(1,128)} %param.10) | copy-start | bytes 12292
  24.1 52.3 %all-to-all-start = ((bf16[64,48,256]{2,1,0:T(8,128)(2,1)}), bf16[64,48,256]{2,1,0:T(8,128)(2,1)}, u32[]{:S(2)}, u32[]{:S(2)}) async-start(bf16[64,48,256]{2,1,0:T(8,128)(2,1)} %bitcast.79), calls=%async_computation | async-start | bytes 3145728 | tf_op jit(solution)/shard_map/all_to_all | solution.py:54
  36.4 89.0 %all-gather.4.cloned.1.call-start = ((), (), s32[]{:S(2)}) async-start(), calls=%async_computation.4 | async-start | bytes 2621440 | tf_op jit(solution)/shard_map/all_gather | solution.py:44
  36.5 4.9 %copy-start.5 = (s32[8,12]{1,0:T(8,128)S(1)}, s32[8,12]{1,0:T(8,128)}, u32[]{:S(2)}) copy-start(s32[8,12]{1,0:T(8,128)} %param.11) | copy-start | bytes 1156
  36.5 5.0 %copy-start.7 = (s32[8]{0:T(128)S(1)}, s32[8]{0:T(128)}, u32[]{:S(2)}) copy-start(s32[8]{0:T(128)} %param.12) | copy-start | bytes 100
  105.6 45.6 %all-to-all-start.1 = ((bf16[64,48,256]{2,1,0:T(8,128)(2,1)}), bf16[64,48,256]{2,1,0:T(8,128)(2,1)}, u32[]{:S(2)}, u32[]{:S(2)}) async-start(bf16[64,48,256]{2,1,0:T(8,128)(2,1)} %bitcast.81), calls=%async_computation.1 | async-start | bytes 3145728 | tf_op jit(solution)/shard_map/all_to_all | solution.py:54
  111.2 89.1 %all-gather.6.cloned.1.call-start = ((), (), s32[]{:S(2)}) async-start(), calls=%async_computation.5 | async-start | bytes 2621440 | tf_op jit(solution)/shard_map/all_gather | solution.py:44
  180.6 45.6 %all-to-all-start.2 = ((bf16[64,48,256]{2,1,0:T(8,128)(2,1)}), bf16[64,48,256]{2,1,0:T(8,128)(2,1)}, u32[]{:S(2)}, u32[]{:S(2)}) async-start(bf16[64,48,256]{2,1,0:T(8,128)(2,1)} %bitcast.80), calls=%async_computation.2 | async-start | bytes 3145728 | tf_op jit(solution)/shard_map/all_to_all | solution.py:54
  186.2 89.1 %all-gather.8.cloned.1.call-start = ((), (), s32[]{:S(2)}) async-start(), calls=%async_computation.6 | async-start | bytes 2621440 | tf_op jit(solution)/shard_map/all_gather | solution.py:44
  242.5 36.2 %copy-start.2 = (bf16[1024,256]{1,0:T(8,128)(2,1)S(1)}, bf16[1024,256]{1,0:T(8,128)(2,1)}, u32[]{:S(2)}) copy-start(bf16[1024,256]{1,0:T(8,128)(2,1)} %fusion.18) | copy-start | bytes 1572868
  242.5 177.8 %reduce-scatter.2.cloned.1.call-start = ((), (), s32[]{:S(2)}) async-start(), calls=%async_computation.7 | async-start | bytes 1064960 | tf_op jit(solution)/shard_map/reduce_scatter | solution.py:69
  290.1 1.5 copy-start.1
  290.1 2.5 copy-start.6
Sparse Core Ops, SparseCore 0:
  92.7 32.6 all-gather.3
  167.7 32.6 all-gather.5
  242.6 32.6 all-gather.7
  279.1 141.0 reduce-scatter.1
where the time goes:
time: 429 us; the launch traced here: 428 us
  waiting for transfers between devices  266 us (62%)
  local copies, waits for them, and re-layouts  83.1 us (19%)
  matrix products  26.9 us (6%)
  starting transfers between devices  23.8 us (6%)
  other arithmetic  14.5 us (3%)
  between operations  14 us (3%)
    reduce_scatter x1, waiting for transfers between devices, body(): lax.psum_scatter(totals[1], 'trainer', scatter_dimension=0, tiled=True)  125 us
    all_to_all x3, waiting for transfers between devices, body(): lax.all_to_all(history[layer_index][send_rows[0]], 'trainer', split_axis=...  79.8 us
    all_gather x3, waiting for transfers between devices, fold_columns(): return add_columns(lax.all_gather(support, 'mp', axis=1, tiled=True))  60.8 us
    gather x3, local copies, waits for them, and re-layouts, body(): history[layer_index][send_rows[0]]  39.7 us
    all_to_all x3, starting transfers between devices, body(): lax.all_to_all(history[layer_index][send_rows[0]], 'trainer', split_axis=...  23.5 us
    gather x3, local copies, waits for them, and re-layouts, aggregate_blocks(): picked = blocks[column_ids]  22.8 us
    dot_general x3, matrix products, aggregate_blocks(): jnp.einsum('rkij,rkjd->rid', masked, picked, preferred_element_type=jnp.f...  14.4 us
    scatter x2, local copies, waits for them, and re-layouts, body(): fresh_rows.append(history[layer_index + 1].at[local_ids].set(current))  11.4 us
  transfers between devices with their start and end apart: 7, of which 7 were waited for; matrix products, arithmetic and copies ran while one was open for 12% of the time, Pallas kernels for 0%

commit v1 on v0

v1 whole, which is shorter than its diff:
```python
import functools
import math

import jax
import jax.numpy as jnp
from jax import lax
from jax.experimental import pallas as pl
from jax.experimental.pallas import tpu as pltpu
from jax.sharding import Mesh
from jax.sharding import PartitionSpec as P

LAYERS = 3
BLK = 128
FEAT = 256
BATCH = 1024
HALO = 3072
HIST = 2048
ROWS = 512
SLOTS = 12
RB = 8
TRAINER = ("z", "x", "core")

mixing = 0.1
strength = 0.5
bf16 = jnp.bfloat16
f32 = jnp.float32

VMEM = pl.BlockSpec(memory_space=pltpu.VMEM)
SMEM = pl.BlockSpec(memory_space=pltpu.SMEM)


def layer_share(layer_index):
    return math.log(strength / (layer_index + 1) + 1.0)


def params(mib):
    return pltpu.CompilerParams(vmem_limit_bytes=mib * 2**20)


def cost(flops, read):
    return pl.CostEstimate(flops=flops, bytes_accessed=read, transcendentals=0)


def one_hot_of(ids):
    at = lax.broadcasted_iota(jnp.int32, (BLK, HIST), 1)
    parts = [(at == ids[:, b : b + 1]).astype(f32).astype(bf16) for b in range(ids.shape[1])]
    return jnp.concatenate(parts, 0)


def pick(chosen, rows):
    return jnp.dot(chosen, rows, preferred_element_type=f32).astype(bf16)


def gather_first_kernel(ids_ref, history_ref, out_ref):
    out_ref[...] = pick(one_hot_of(ids_ref[0]), history_ref[0])


def gather_first(ids, history):
    steps = HALO // ROWS
    return pl.pallas_call(
        gather_first_kernel,
        grid=(steps,),
        in_specs=[
            pl.BlockSpec((1, BLK, ROWS // BLK), lambda i: (i, 0, 0)),
            pl.BlockSpec((1, HIST, FEAT), lambda i: (0, 0, 0)),
        ],
        out_specs=pl.BlockSpec((ROWS, FEAT), lambda i: (i, 0)),
        out_shape=jax.ShapeDtypeStruct((HALO, FEAT), bf16),
        compiler_params=params(32),
        cost_estimate=cost(2 * HALO * HIST * FEAT, 3 << 20),
        name="gather_first",
    )(ids, history)


def gather_rest_kernel(ids_ref, history_ref, one_ref, two_ref, start_ref):
    step = pl.program_id(0)
    chosen = one_hot_of(ids_ref[0])

    @pl.when(step >= 2)
    def _():
        one_ref[...] = pick(chosen, history_ref[1])
        two_ref[...] = pick(chosen, history_ref[2])

    @pl.when(step < 2)
    def _():
        start_ref[...] = pick(chosen, history_ref[0])


def gather_rest(ids, history):
    steps = (HALO + BATCH) // ROWS
    late = lambda i: (jnp.maximum(i - 2, 0), 0)
    return pl.pallas_call(
        gather_rest_kernel,
        grid=(steps,),
        in_specs=[
            pl.BlockSpec((1, BLK, ROWS // BLK), lambda i: (i, 0, 0)),
            pl.BlockSpec((LAYERS, HIST, FEAT), lambda i: (0, 0, 0)),
        ],
        out_specs=[
            pl.BlockSpec((ROWS, FEAT), late),
            pl.BlockSpec((ROWS, FEAT), late),
            pl.BlockSpec((ROWS, FEAT), lambda i: (jnp.minimum(i, 1), 0)),
        ],
        out_shape=[
            jax.ShapeDtypeStruct((HALO, FEAT), bf16),
            jax.ShapeDtypeStruct((HALO, FEAT), bf16),
            jax.ShapeDtypeStruct((BATCH, FEAT), bf16),
        ],
        compiler_params=params(32),
        cost_estimate=cost(2 * (2 * HALO + BATCH) * HIST * FEAT, 6 << 20),
        name="gather_rest",
    )(ids, history)


def aggregate_kernel(cols_ref, count_ref, rows_ref, halo_ref, start_ref, adj_ref, out_ref, x_ref, picked_ref):
    x_ref[:RB] = rows_ref[...].reshape(RB, BLK, FEAT)
    x_ref[RB:] = halo_ref[...].reshape(HALO // BLK, BLK, FEAT)

    @pl.loop(0, RB)
    def _(r):
        count = count_ref[r]
        parts = []
        for k in range(SLOTS):
            picked_ref[k * BLK : (k + 1) * BLK, :] = x_ref[cols_ref[r, k]]
            block = adj_ref[r, k]
            parts.append(jnp.where(k < count, block, jnp.zeros_like(block)))
        total = jnp.dot(jnp.concatenate(parts, 1), picked_ref[...], preferred_element_type=f32)
        at = pl.ds(pl.multiple_of(r * BLK, BLK), BLK)
        start = start_ref[at, :].astype(f32)
        out_ref[at, :] = ((1.0 - mixing) * total + mixing * start).astype(bf16)


def aggregate(cols, count, rows, halo, start, adjacency):
    return pl.pallas_call(
        aggregate_kernel,
        in_specs=[SMEM, SMEM, VMEM, VMEM, VMEM, VMEM],
        out_specs=VMEM,
        out_shape=jax.ShapeDtypeStruct((BATCH, FEAT), bf16),
        scratch_shapes=[
            pltpu.VMEM((RB + HALO // BLK, BLK, FEAT), bf16),
            pltpu.VMEM((SLOTS * BLK, FEAT), bf16),
        ],
        compiler_params=params(32),
        cost_estimate=cost(2 * BATCH * SLOTS * BLK * FEAT, 6 << 20),
        name="aggregate",
    )(cols, count, rows, halo, start, adjacency)


def shift(array, axis, size, by):
    return lax.ppermute(array, axis, [(i, (i + by) % size) for i in range(size)])


def ring_gather(rows):
    half = rows.shape[0] // 2
    up, low = rows[:half], rows[half:]
    left_up, right_low = shift(up, "y", 4, 1), shift(low, "y", 4, 3)
    left_low, right_up = shift(low, "y", 4, 1), shift(up, "y", 4, 3)
    far_up, far_low = shift(left_up, "y", 4, 1), shift(right_low, "y", 4, 3)
    return left_up, left_low, right_up, right_low, far_up, far_low


def mix_kernel(share, last, me_ref, own_ref, lu_ref, ll_ref, ru_ref, rl_ref, fu_ref, fl_ref, w_ref, out_ref):
    me = me_ref[0]

    def slab(by):
        at = lax.rem(me + by, 4) * FEAT
        return w_ref[0, pl.ds(pl.multiple_of(at, FEAT), FEAT), :]

    half = BATCH // 2
    for part, others in ((0, (lu_ref, ru_ref, fu_ref)), (1, (ll_ref, rl_ref, fl_ref))):
        at = slice(part * half, (part + 1) * half)
        own = own_ref[at, :]
        total = jnp.dot(own, slab(0), preferred_element_type=f32)
        for other, by in zip(others, (3, 1, 2)):
            total += jnp.dot(other[...], slab(by), preferred_element_type=f32)
        mixed = (1.0 - share) * own.astype(f32) + share * total
        out_ref[at, :] = (mixed if last else jnp.maximum(mixed, 0.0)).astype(bf16)


def mix(layer_index, me, support, others, weights):
    last = layer_index + 1 == LAYERS
    whole = lambda shape: pl.BlockSpec(shape, lambda i: (0,) * len(shape))
    return pl.pallas_call(
        functools.partial(mix_kernel, layer_share(layer_index), last),
        grid=(1,),
        in_specs=[SMEM, whole((BATCH, FEAT))]
        + [whole((BATCH // 2, FEAT))] * 6
        + [pl.BlockSpec((1, 4 * FEAT, FEAT), lambda i: (layer_index, 0, 0))],
        out_specs=whole((BATCH, FEAT)),
        out_shape=jax.ShapeDtypeStruct((BATCH, FEAT), bf16),
        compiler_params=params(32),
        cost_estimate=cost(2 * BATCH * 4 * FEAT * FEAT, 3 << 20),
        name="mix",
    )(me, support, *others, weights)


def write_kernel(ids_ref, history_ref, one_ref, two_ref, out_ref):
    base = pl.program_id(0) * ROWS
    at = lax.broadcasted_iota(jnp.int32, (ROWS, BATCH), 0) + base
    chosen = (at == ids_ref[...]).astype(f32)
    hit = jnp.max(chosen, axis=1, keepdims=True) > 0.0
    chosen = chosen.astype(bf16)
    for layer, rows in ((0, one_ref), (1, two_ref)):
        put = pick(chosen, rows[...])
        out_ref[layer] = jnp.where(hit, put, history_ref[layer + 1])


def write_rows(ids, history, one, two):
    return pl.pallas_call(
        write_kernel,
        grid=(HIST // ROWS,),
        in_specs=[
            pl.BlockSpec((1, BATCH), lambda i: (0, 0)),
            pl.BlockSpec((LAYERS, ROWS, FEAT), lambda i: (0, i, 0)),
            pl.BlockSpec((BATCH, FEAT), lambda i: (0, 0)),
            pl.BlockSpec((BATCH, FEAT), lambda i: (0, 0)),
        ],
        out_specs=pl.BlockSpec((2, ROWS, FEAT), lambda i: (0, i, 0)),
        out_shape=jax.ShapeDtypeStruct((2, HIST, FEAT), bf16),
        compiler_params=params(32),
        cost_estimate=cost(4 * BATCH * HIST * FEAT, 6 << 20),
        name="write_rows",
    )(ids, history, one, two)


def grad_kernel(core_ref, support_ref, cot_ref, keep_ref, send_ref, acc_ref):
    support = support_ref[...]
    for part in range(4):
        acc_ref[:, :, part * FEAT : (part + 1) * FEAT] = lax.dot_general(
            support, cot_ref[part], (((0,), (0,)), ((), ())), preferred_element_type=f32
        ).reshape(8, 32, FEAT)
    mine = pl.multiple_of(core_ref[0] * 16, 16)
    theirs = pl.multiple_of(16 - core_ref[0] * 16, 16)
    for group in range(8):
        keep_ref[group] = acc_ref[group, pl.ds(mine, 16), :]
        send_ref[group] = acc_ref[group, pl.ds(theirs, 16), :]


def grad_terms(core, support, cotangent):
    return pl.pallas_call(
        grad_kernel,
        in_specs=[SMEM, VMEM, VMEM],
        out_specs=[VMEM, VMEM],
        out_shape=[jax.ShapeDtypeStruct((8, 16, 4 * FEAT), f32)] * 2,
        scratch_shapes=[pltpu.VMEM((8, 32, 4 * FEAT), f32)],
        compiler_params=params(32),
        cost_estimate=cost(2 * BATCH * FEAT * 4 * FEAT, 4 << 20),
        name="grad_terms",
    )(core, support, cotangent)


def reduce_grad(keep, send):
    total = keep + shift(send, "core", 2, 1)
    total = total.reshape(2, 4, 16, 4, FEAT).transpose(1, 3, 0, 2, 4).reshape(16, 32, FEAT)
    total = lax.all_to_all(total, ("x", "y"), 0, 0, tiled=True)
    total = total.reshape(4, 8, 16, FEAT).sum(0)
    total = lax.all_to_all(total, "z", 0, 0, tiled=True)
    return total.sum(0) * layer_share(LAYERS - 1)


def body(history, send_rows, batch_ids, block_cols, block_count, adjacency, weights, cotangent):
    me = lax.axis_index("y").astype(jnp.int32).reshape(1)
    core = lax.axis_index("core").astype(jnp.int32).reshape(1)
    by_step = lambda ids: ids.reshape(-1, ROWS // BLK, BLK).transpose(0, 2, 1)
    send_ids = by_step(send_rows)
    batch = by_step(batch_ids)

    def exchange(rows):
        rows = rows.reshape(64, HALO // 64, FEAT)
        return lax.all_to_all(rows, TRAINER, 0, 0, tiled=True).reshape(HALO, FEAT)

    halo_0 = exchange(gather_first(send_ids, history))
    send_1, send_2, start = gather_rest(jnp.concatenate([batch, send_ids], 0), history)
    halo_1 = exchange(send_1)
    halo_2 = exchange(send_2)
    cot_all = lax.all_gather(cotangent, "y", axis=0, tiled=False)

    support = aggregate(block_cols, block_count, start, halo_0, start, adjacency)
    one = mix(0, me, support, ring_gather(support), weights)
    support = aggregate(block_cols, block_count, one, halo_1, start, adjacency)
    two = mix(1, me, support, ring_gather(support), weights)
    fresh = write_rows(batch_ids, history, one, two)
    support = aggregate(block_cols, block_count, two, halo_2, start, adjacency)
    grad = reduce_grad(*grad_terms(core, support, cot_all))
    final = mix(2, me, support, ring_gather(support), weights)
    return fresh, final, grad


def solution(mesh):
    fine = Mesh(mesh.devices.reshape(8, 4, 2, 4), ("z", "x", "core", "y"))
    return jax.shard_map(
        body,
        mesh=fine,
        in_specs=(
            P(None, TRAINER, "y"),
            P(TRAINER, None, None),
            P(TRAINER, None),
            P(TRAINER, None),
            P(TRAINER),
            P(TRAINER, None, None, None),
            P(None, None, "y"),
            P(TRAINER, "y"),
        ),
        out_specs=(P(None, TRAINER, "y"), P(TRAINER, "y"), P(TRAINER, "y")),
        check_vma=False,
    )
```

time: 429 us -> 258 us (0.60)
  waiting for transfers between devices: 266 us -> 72.6 us
  local copies, waits for them, and re-layouts: 83.1 us -> 27.8 us
  blocking collectives: 0 us -> 45.4 us
  Pallas kernels: 0 us -> 39.1 us
  starting transfers between devices: 23.8 us -> 52.6 us
  matrix products: 26.9 us -> 0 us
  other arithmetic: 14.5 us -> 2.45 us
    reduce_scatter x1 -> x0, waiting for transfers between devices: 125 us -> none  [body(): lax.psum_scatter(totals[1], 'trainer', scatter_dimension=0, tiled=True)]
    gather x7 -> x0, local copies, waits for them, and re-layouts: 67.3 us -> none  [the longest x3 39.7 us: body(): history[layer_index][send_rows[0]]]
    all_gather x3 -> x1, waiting for transfers between devices: 60.8 us -> 0.01 us  [body(): cot_all = lax.all_gather(cotangent, 'y', axis=0, tiled=False)]
    all_to_all x3 -> x4, waiting for transfers between devices: 79.8 us -> 24 us  [the longest x2 22.6 us: exchange(): return lax.all_to_all(rows, TRAINER, 0, 0, tiled=True).reshape(HALO, FEAT)]
    ppermute x0 -> x19, waiting for transfers between devices: none -> 47.9 us  [shift(): lax.ppermute(array, axis, [(i, (i + by) % size) for i in range(size)])]
    all_to_all x0 -> x1, blocking collectives: none -> 45.4 us  [exchange(): return lax.all_to_all(rows, TRAINER, 0, 0, tiled=True).reshape(HALO, FEAT)]
    pallas_call x0 -> x10, Pallas kernels: none -> 39.1 us  [the longest x1 13.5 us: gather_rest(): pl.pallas_call(gather_rest_kernel, grid=(steps,), in_specs=[pl.BlockSpec(...]
    dot_general x7 -> x0, matrix products: 26.9 us -> none  [the longest x3 14.4 us: aggregate_blocks(): jnp.einsum('rkij,rkjd->rid', masked, picked, preferred_element_type=jnp.f...]
  transfers between devices with their start and end apart: 7 -> 24, of which waited for: 7 -> 16; matrix products, arithmetic and copies ran while one was open for 12% -> 2% of each run, Pallas kernels for 0% -> 13%
where the time goes in v1:
time: 258 us; the launch traced here: 254 us
  waiting for transfers between devices  72.6 us (28%)
  starting transfers between devices  52.6 us (20%)
  blocking collectives  45.4 us (18%)
  Pallas kernels  39.1 us (15%)
  local copies, waits for them, and re-layouts  27.8 us (11%)
  between operations  14.4 us (6%)
    ppermute x19, waiting for transfers between devices, shift(): lax.ppermute(array, axis, [(i, (i + by) % size) for i in range(size)])  47.9 us
    all_to_all x1, blocking collectives, exchange(): return lax.all_to_all(rows, TRAINER, 0, 0, tiled=True).reshape(HALO, FEAT)  45.4 us
    unnamed x63, local copies, waits for them, and re-layouts  23.7 us
    all_to_all x2, waiting for transfers between devices, exchange(): return lax.all_to_all(rows, TRAINER, 0, 0, tiled=True).reshape(HALO, FEAT)  22.6 us
    ppermute x19, starting transfers between devices, shift(): lax.ppermute(array, axis, [(i, (i + by) % size) for i in range(size)])  19.1 us
    all_to_all x2, starting transfers between devices, exchange(): return lax.all_to_all(rows, TRAINER, 0, 0, tiled=True).reshape(HALO, FEAT)  17.9 us
    pallas_call x1, Pallas kernels, gather_rest(): pl.pallas_call(gather_rest_kernel, grid=(steps,), in_specs=[pl.BlockSpec(...  13.5 us
    pallas_call x3, Pallas kernels, aggregate(): pl.pallas_call(aggregate_kernel, in_specs=[SMEM, SMEM, VMEM, VMEM, VMEM,...  9.7 us
  transfers between devices with their start and end apart: 24, of which 16 were waited for; matrix products, arithmetic and copies ran while one was open for 2% of the time, Pallas kernels for 13%

profile of v1, /device:TPU:8, one launch (start us, length us, event | category | flops | bytes accessed | tf_op | source)
XLA Modules:
  0.0 254.4 jit_solution(12676520045761119710)
XLA Ops:
  8.3 1.9 copy-done.28
  10.2 5.3 %gather_first.1 = bf16[3072,256]{1,0:T(8,128)(2,1)} custom-call(s32[6,128,4]{2,1,0:T(8,128)S(1)} %bitcast.21, bf16[3,2048,256]{2,1,0:T(8,128)(2,1)S(1)} %copy-done.28), custom_call_target="tpu_custom_call" | custom-call | flops 3221225472 | bytes 3145728 | tf_op jit(solution)/shard_map/gather_first/pallas_call | solution.py:60
  15.5 12.1 %all-to-all-start = ((bf16[64,48,256]{2,1,0:T(8,128)(2,1)}), bf16[64,48,256]{2,1,0:T(8,128)(2,1)S(1)}, u32[]{:S(2)}, u32[]{:S(2)}) async-start(bf16[64,48,256]{2,1,0:T(8,128)(2,1)} %bitcast.4), calls=%async_computation | async-start | bytes 3145728 | tf_op jit(solution)/shard_map/all_to_all | solution.py:270
  27.8 1.9 copy-done.29
  29.6 13.5 %gather_rest.1 = (bf16[3072,256]{1,0:T(8,128)(2,1)S(1)}, bf16[3072,256]{1,0:T(8,128)(2,1)S(1)}, bf16[1024,256]{1,0:T(8,128)(2,1)S(1)}) custom-call(s32[8,128,4]{2,1,0:T(8,128)S(1)} %pad_add_fusion.ids_ref, bf16[3,2048,256]{2,1,0:T(8,128)(2,1)S(1)} %copy-done.29), custom_call_target="tpu_custom_call" | custom-call | flops 7516192768 | bytes 6291456 | tf_op jit(solution)/shard_map/gather_rest/pallas_call | solution.py:92
  45.1 22.6 %all-to-all-done = bf16[64,48,256]{2,1,0:T(8,128)(2,1)S(1)} async-done(((bf16[64,48,256]{2,1,0:T(8,128)(2,1)}), bf16[64,48,256]{2,1,0:T(8,128)(2,1)S(1)}, u32[]{:S(2)}, u32[]{:S(2)}) %all-to-all-start) | async-done | bytes 1572896 | tf_op jit(solution)/shard_map/all_to_all | solution.py:270
  67.7 45.4 %all_to_all.25 = bf16[64,48,256]{2,1,0:T(8,128)(2,1)} all-to-all(bf16[64,48,256]{2,1,0:T(8,128)(2,1)S(1)} %bitcast.20), channel_id=1, replica_groups=mesh['z'=8,'x'=4,'core'=2,'y'=4] {'z','x','core'}, dimensions={0} | all-to-all | bytes 3145728 | tf_op jit(solution)/shard_map/all_to_all | solution.py:270
  113.0 5.8 %all-to-all-start.2 = ((bf16[64,48,256]{2,1,0:T(8,128)(2,1)}), bf16[64,48,256]{2,1,0:T(8,128)(2,1)}, u32[]{:S(2)}, u32[]{:S(2)}) async-start(bf16[64,48,256]{2,1,0:T(8,128)(2,1)} %bitcast.19), calls=%async_computation.2 | async-start | bytes 3145728 | tf_op jit(solution)/shard_map/all_to_all | solution.py:270
  122.1 3.0 %aggregate.3.own_ref = bf16[1024,256]{1,0:T(8,128)(2,1)S(1)} custom-call(s32[8,12]{1,0:T(8,128)S(1)} %copy-done.25, s32[8]{0:T(128)S(1)} %copy-done.26, bf16[1024,256]{1,0:T(8,128)(2,1)S(1)} %copy-done.5, bf16[3072,256]{1,0:T(8,128)(2,1)S(1)} %bitcast.17, bf16[1024,256]{1,0:T(8,128)(2,1)S(1)} %copy-done.5, bf16[8,12,128,128]{3,2,1,0:T(8,128)(2,1)S(1)} %copy-done), custom_call_target="tpu_custom_call" | custom-call | flops 805306368 | bytes 6291456 | tf_op jit(solution)/shard_map/aggregate/pallas_call | solution.py:134
  130.8 5.3 %collective-permute-done.lu_ref = bf16[512,256]{1,0:T(8,128)(2,1)S(1)} collective-permute-done((bf16[512,256]{1,0:T(8,128)(2,1)}, bf16[512,256]{1,0:T(8,128)(2,1)S(1)}, u32[]{:S(2)}, u32[]{:S(2)}) %collective-permute-start) | collective-permute-done | bytes 262176 | tf_op jit(solution)/shard_map/ppermute | solution.py:150
  138.3 8.5 %collective-permute-done.1.ll_ref = bf16[512,256]{1,0:T(8,128)(2,1)} collective-permute-done((bf16[512,256]{1,0:T(8,128)(2,1)}, bf16[512,256]{1,0:T(8,128)(2,1)}, u32[]{:S(2)}, u32[]{:S(2)}) %collective-permute-start.1) | collective-permute-done | bytes 262176 | tf_op jit(solution)/shard_map/ppermute | solution.py:150
  146.8 1.9 collective-permute-done.2.ru_ref
  148.7 8.4 %collective-permute-done.4.fu_ref = bf16[512,256]{1,0:T(8,128)(2,1)} collective-permute-done((bf16[512,256]{1,0:T(8,128)(2,1)S(1)}, bf16[512,256]{1,0:T(8,128)(2,1)}, u32[]{:S(2)}, u32[]{:S(2)}) %collective-permute-start.4) | collective-permute-done | bytes 262176 | tf_op jit(solution)/shard_map/ppermute | solution.py:150
  161.1 2.1 mix.3.rows_ref.one_ref
  163.3 3.0 %aggregate.4.own_ref = bf16[1024,256]{1,0:T(8,128)(2,1)S(1)} custom-call(s32[8,12]{1,0:T(8,128)S(1)} %copy-done.25, s32[8]{0:T(128)S(1)} %copy-done.26, bf16[1024,256]{1,0:T(8,128)(2,1)S(1)} %mix.3.rows_ref.one_ref, bf16[3072,256]{1,0:T(8,128)(2,1)S(1)} %bitcast.16, bf16[1024,256]{1,0:T(8,128)(2,1)S(1)} %copy-done.6, bf16[8,12,128,128]{3,2,1,0:T(8,128)(2,1)S(1)} %copy-done), custom_call_target="tpu_custom_call" | custom-call | flops 805306368 | bytes 6291456 | tf_op jit(solution)/shard_map/aggregate/pallas_call | solution.py:134
  172.4 5.0 %collective-permute-done.6.lu_ref = bf16[512,256]{1,0:T(8,128)(2,1)S(1)} collective-permute-done((bf16[512,256]{1,0:T(8,128)(2,1)}, bf16[512,256]{1,0:T(8,128)(2,1)S(1)}, u32[]{:S(2)}, u32[]{:S(2)}) %collective-permute-start.6) | collective-permute-done | bytes 262176 | tf_op jit(solution)/shard_map/ppermute | solution.py:150
  181.2 2.1 collective-permute-done.8.ru_ref
  188.5 2.0 mix.4.two_ref.rows_ref
  193.4 3.8 %aggregate.5.own_ref.support_ref = bf16[1024,256]{1,0:T(8,128)(2,1)S(1)} custom-call(s32[8,12]{1,0:T(8,128)S(1)} %copy-done.25, s32[8]{0:T(128)S(1)} %copy-done.26, bf16[1024,256]{1,0:T(8,128)(2,1)S(1)} %copy-done.21, bf16[3072,256]{1,0:T(8,128)(2,1)} %bitcast.9.halo_ref, bf16[1024,256]{1,0:T(8,128)(2,1)S(1)} %copy-done.7, bf16[8,12,128,128]{3,2,1,0:T(8,128)(2,1)S(1)} %copy-done), custom_call_target="tpu_custom_call" | custom-call | flops 805306368 | bytes 6291456 | tf_op jit(solution)/shard_map/aggregate/pallas_call | solution.py:134
  201.6 1.9 collective-permute-done.18
  204.7 9.0 %all-to-all-start.3 = ((f32[16,32,256]{2,1,0:T(8,128)}), f32[16,32,256]{2,1,0:T(8,128)}, u32[]{:S(2)}, u32[]{:S(2)}) async-start(f32[16,32,256]{2,1,0:T(8,128)} %bitcast.13), calls=%async_computation.3 | async-start | bytes 1048576 | tf_op jit(solution)/shard_map/all_to_all | solution.py:255
  218.5 8.5 %collective-permute-done.12.lu_ref = bf16[512,256]{1,0:T(8,128)(2,1)S(1)} collective-permute-done((bf16[512,256]{1,0:T(8,128)(2,1)}, bf16[512,256]{1,0:T(8,128)(2,1)S(1)}, u32[]{:S(2)}, u32[]{:S(2)}) %collective-permute-start.12) | collective-permute-done | bytes 262176 | tf_op jit(solution)/shard_map/ppermute | solution.py:150
  231.2 6.6 %all-to-all-start.4 = ((f32[8,16,256]{2,1,0:T(8,128)}), f32[8,16,256]{2,1,0:T(8,128)S(1)}, u32[]{:S(2)}, u32[]{:S(2)}) async-start(f32[8,16,256]{2,1,0:T(8,128)} %reduce_sum.18), calls=%async_computation.4 | async-start | bytes 262144 | tf_op jit(solution)/shard_map/all_to_all | solution.py:257
  239.7 4.2 %write_rows.1 = bf16[2,2048,256]{2,1,0:T(8,128)(2,1)} custom-call(s32[1,1024]{1,0:T(1,128)S(1)} %copy-done.27, bf16[3,2048,256]{2,1,0:T(8,128)(2,1)S(1)} %copy-done.30, bf16[1024,256]{1,0:T(8,128)(2,1)S(1)} %copy-done.19, bf16[1024,256]{1,0:T(8,128)(2,1)S(1)} %copy-done.22), custom_call_target="tpu_custom_call" | custom-call | flops 2147483648 | bytes 6291456 | tf_op jit(solution)/shard_map/write_rows/pallas_call | solution.py:209
  (112 shorter events, 56.4 us)
Async XLA Ops:
  15.5 52.2 %all-to-all-start = ((bf16[64,48,256]{2,1,0:T(8,128)(2,1)}), bf16[64,48,256]{2,1,0:T(8,128)(2,1)S(1)}, u32[]{:S(2)}, u32[]{:S(2)}) async-start(bf16[64,48,256]{2,1,0:T(8,128)(2,1)} %bitcast.4), calls=%async_computation | async-start | bytes 3145728 | tf_op jit(solution)/shard_map/all_to_all | solution.py:270
  113.0 78.3 %all-to-all-start.2 = ((bf16[64,48,256]{2,1,0:T(8,128)(2,1)}), bf16[64,48,256]{2,1,0:T(8,128)(2,1)}, u32[]{:S(2)}, u32[]{:S(2)}) async-start(bf16[64,48,256]{2,1,0:T(8,128)(2,1)} %bitcast.19), calls=%async_computation.2 | async-start | bytes 3145728 | tf_op jit(solution)/shard_map/all_to_all | solution.py:270
  118.9 79.1 %all-gather.3.cloned.1.call-start = ((), (), s32[]{:S(2)}) async-start(), calls=%async_computation.5 | async-start | bytes 2621440 | tf_op jit(solution)/shard_map/all_gather | solution.py:276
  126.7 9.4 %collective-permute-start = (bf16[512,256]{1,0:T(8,128)(2,1)}, bf16[512,256]{1,0:T(8,128)(2,1)S(1)}, u32[]{:S(2)}, u32[]{:S(2)}) collective-permute-start(bf16[512,256]{1,0:T(8,128)(2,1)} %get-tuple-element.18), channel_id=1, source_target_pairs={{0,1},{1,2},{2,3},{3,0},{4,5},{5,6},{6,7},{7,4},{8,9},{9,10},{10,1... | collective-permute-start | bytes 786440 | tf_op jit(solution)/shard_map/ppermute | solution.py:150
  128.3 9.5 %collective-permute-start.3 = (bf16[512,256]{1,0:T(8,128)(2,1)}, bf16[512,256]{1,0:T(8,128)(2,1)}, u32[]{:S(2)}, u32[]{:S(2)}) collective-permute-start(bf16[512,256]{1,0:T(8,128)(2,1)} %get-tuple-element.17), channel_id=1, source_target_pairs={{0,3},{1,0},{2,1},{3,2},{4,7},{5,4},{6,5},{7,6},{8,11},{9,8},{10,9... | collective-permute-start | bytes 786440 | tf_op jit(solution)/shard_map/ppermute | solution.py:150
  128.7 18.1 %collective-permute-start.1 = (bf16[512,256]{1,0:T(8,128)(2,1)}, bf16[512,256]{1,0:T(8,128)(2,1)}, u32[]{:S(2)}, u32[]{:S(2)}) collective-permute-start(bf16[512,256]{1,0:T(8,128)(2,1)} %get-tuple-element.17), channel_id=1, source_target_pairs={{0,1},{1,2},{2,3},{3,0},{4,5},{5,6},{6,7},{7,4},{8,9},{9,10},{10,1... | collective-permute-start | bytes 786440 | tf_op jit(solution)/shard_map/ppermute | solution.py:150
  130.3 18.4 %collective-permute-start.2 = (bf16[512,256]{1,0:T(8,128)(2,1)}, bf16[512,256]{1,0:T(8,128)(2,1)}, u32[]{:S(2)}, u32[]{:S(2)}) collective-permute-start(bf16[512,256]{1,0:T(8,128)(2,1)} %get-tuple-element.18), channel_id=1, source_target_pairs={{0,3},{1,0},{2,1},{3,2},{4,7},{5,4},{6,5},{7,6},{8,11},{9,8},{10,9... | collective-permute-start | bytes 786440 | tf_op jit(solution)/shard_map/ppermute | solution.py:150
  136.1 21.0 %collective-permute-start.4 = (bf16[512,256]{1,0:T(8,128)(2,1)S(1)}, bf16[512,256]{1,0:T(8,128)(2,1)}, u32[]{:S(2)}, u32[]{:S(2)}) collective-permute-start(bf16[512,256]{1,0:T(8,128)(2,1)S(1)} %collective-permute-done.lu_ref), channel_id=1, source_target_pairs={{0,1},{1,2},{2,3},{3,0},{4,5},{5,6},{6,7},{7,4},{8,9},{9,10},{10,1... | collective-permute-start | bytes 786440 | tf_op jit(solution)/shard_map/ppermute | solution.py:150
  137.8 20.8 %collective-permute-start.5 = (bf16[512,256]{1,0:T(8,128)(2,1)}, bf16[512,256]{1,0:T(8,128)(2,1)}, u32[]{:S(2)}, u32[]{:S(2)}) collective-permute-start(bf16[512,256]{1,0:T(8,128)(2,1)} %collective-permute-done.3.rl_ref), channel_id=1, source_target_pairs={{0,3},{1,0},{2,1},{3,2},{4,7},{5,4},{6,5},{7,6},{8,11},{9,8},{10,9... | collective-permute-start | bytes 786440 | tf_op jit(solution)/shard_map/ppermute | solution.py:150
  167.9 9.5 %collective-permute-start.6 = (bf16[512,256]{1,0:T(8,128)(2,1)}, bf16[512,256]{1,0:T(8,128)(2,1)S(1)}, u32[]{:S(2)}, u32[]{:S(2)}) collective-permute-start(bf16[512,256]{1,0:T(8,128)(2,1)} %get-tuple-element.16), channel_id=1, source_target_pairs={{0,1},{1,2},{2,3},{3,0},{4,5},{5,6},{6,7},{7,4},{8,9},{9,10},{10,1... | collective-permute-start | bytes 786440 | tf_op jit(solution)/shard_map/ppermute | solution.py:150
  169.3 10.0 %collective-permute-start.9 = (bf16[512,256]{1,0:T(8,128)(2,1)}, bf16[512,256]{1,0:T(8,128)(2,1)}, u32[]{:S(2)}, u32[]{:S(2)}) collective-permute-start(bf16[512,256]{1,0:T(8,128)(2,1)} %get-tuple-element.15), channel_id=1, source_target_pairs={{0,3},{1,0},{2,1},{3,2},{4,7},{5,4},{6,5},{7,6},{8,11},{9,8},{10,9... | collective-permute-start | bytes 786440 | tf_op jit(solution)/shard_map/ppermute | solution.py:150
  170.0 11.2 %collective-permute-start.7 = (bf16[512,256]{1,0:T(8,128)(2,1)}, bf16[512,256]{1,0:T(8,128)(2,1)}, u32[]{:S(2)}, u32[]{:S(2)}) collective-permute-start(bf16[512,256]{1,0:T(8,128)(2,1)} %get-tuple-element.15), channel_id=1, source_target_pairs={{0,1},{1,2},{2,3},{3,0},{4,5},{5,6},{6,7},{7,4},{8,9},{9,10},{10,1... | collective-permute-start | bytes 786440 | tf_op jit(solution)/shard_map/ppermute | solution.py:150
  171.8 11.4 %collective-permute-start.8 = (bf16[512,256]{1,0:T(8,128)(2,1)}, bf16[512,256]{1,0:T(8,128)(2,1)}, u32[]{:S(2)}, u32[]{:S(2)}) collective-permute-start(bf16[512,256]{1,0:T(8,128)(2,1)} %get-tuple-element.16), channel_id=1, source_target_pairs={{0,3},{1,0},{2,1},{3,2},{4,7},{5,4},{6,5},{7,6},{8,11},{9,8},{10,9... | collective-permute-start | bytes 786440 | tf_op jit(solution)/shard_map/ppermute | solution.py:150
  177.4 6.9 %collective-permute-start.10 = (bf16[512,256]{1,0:T(8,128)(2,1)S(1)}, bf16[512,256]{1,0:T(8,128)(2,1)}, u32[]{:S(2)}, u32[]{:S(2)}) collective-permute-start(bf16[512,256]{1,0:T(8,128)(2,1)S(1)} %collective-permute-done.6.lu_ref), channel_id=1, source_target_pairs={{0,1},{1,2},{2,3},{3,0},{4,5},{5,6},{6,7},{7,4},{8,9},{9,10},{10,1... | collective-permute-start | bytes 786440 | tf_op jit(solution)/shard_map/ppermute | solution.py:150
  179.4 6.7 %collective-permute-start.11 = (bf16[512,256]{1,0:T(8,128)(2,1)}, bf16[512,256]{1,0:T(8,128)(2,1)}, u32[]{:S(2)}, u32[]{:S(2)}) collective-permute-start(bf16[512,256]{1,0:T(8,128)(2,1)} %collective-permute-done.9.rl_ref), channel_id=1, source_target_pairs={{0,3},{1,0},{2,1},{3,2},{4,7},{5,4},{6,5},{7,6},{8,11},{9,8},{10,9... | collective-permute-start | bytes 786440 | tf_op jit(solution)/shard_map/ppermute | solution.py:150
  201.5 2.0 collective-permute-start.18
  204.7 24.8 %all-to-all-start.3 = ((f32[16,32,256]{2,1,0:T(8,128)}), f32[16,32,256]{2,1,0:T(8,128)}, u32[]{:S(2)}, u32[]{:S(2)}) async-start(f32[16,32,256]{2,1,0:T(8,128)} %bitcast.13), calls=%async_computation.3 | async-start | bytes 1048576 | tf_op jit(solution)/shard_map/all_to_all | solution.py:255
  214.5 12.6 %collective-permute-start.12 = (bf16[512,256]{1,0:T(8,128)(2,1)}, bf16[512,256]{1,0:T(8,128)(2,1)S(1)}, u32[]{:S(2)}, u32[]{:S(2)}) collective-permute-start(bf16[512,256]{1,0:T(8,128)(2,1)} %get-tuple-element.14), channel_id=1, source_target_pairs={{0,1},{1,2},{2,3},{3,0},{4,5},{5,6},{6,7},{7,4},{8,9},{9,10},{10,1... | collective-permute-start | bytes 786440 | tf_op jit(solution)/shard_map/ppermute | solution.py:150
  216.0 12.9 %collective-permute-start.15 = (bf16[512,256]{1,0:T(8,128)(2,1)}, bf16[512,256]{1,0:T(8,128)(2,1)S(1)}, u32[]{:S(2)}, u32[]{:S(2)}) collective-permute-start(bf16[512,256]{1,0:T(8,128)(2,1)} %get-tuple-element.13), channel_id=1, source_target_pairs={{0,3},{1,0},{2,1},{3,2},{4,7},{5,4},{6,5},{7,6},{8,11},{9,8},{10,9... | collective-permute-start | bytes 786440 | tf_op jit(solution)/shard_map/ppermute | solution.py:150
  216.5 27.4 %collective-permute-start.13 = (bf16[512,256]{1,0:T(8,128)(2,1)}, bf16[512,256]{1,0:T(8,128)(2,1)S(1)}, u32[]{:S(2)}, u32[]{:S(2)}) collective-permute-start(bf16[512,256]{1,0:T(8,128)(2,1)} %get-tuple-element.13), channel_id=1, source_target_pairs={{0,1},{1,2},{2,3},{3,0},{4,5},{5,6},{6,7},{7,4},{8,9},{9,10},{10,1... | collective-permute-start | bytes 786440 | tf_op jit(solution)/shard_map/ppermute | solution.py:150
  218.0 25.9 %collective-permute-start.14 = (bf16[512,256]{1,0:T(8,128)(2,1)}, bf16[512,256]{1,0:T(8,128)(2,1)S(1)}, u32[]{:S(2)}, u32[]{:S(2)}) collective-permute-start(bf16[512,256]{1,0:T(8,128)(2,1)} %get-tuple-element.14), channel_id=1, source_target_pairs={{0,3},{1,0},{2,1},{3,2},{4,7},{5,4},{6,5},{7,6},{8,11},{9,8},{10,9... | collective-permute-start | bytes 786440 | tf_op jit(solution)/shard_map/ppermute | solution.py:150
  227.1 16.8 %collective-permute-start.16 = (bf16[512,256]{1,0:T(8,128)(2,1)S(1)}, bf16[512,256]{1,0:T(8,128)(2,1)S(1)}, u32[]{:S(2)}, u32[]{:S(2)}) collective-permute-start(bf16[512,256]{1,0:T(8,128)(2,1)S(1)} %collective-permute-done.12.lu_ref), channel_id=1, source_target_pairs={{0,1},{1,2},{2,3},{3,0},{4,5},{5,6},{6,7},{7,4},{8,9},{9,10},{10,1... | collective-permute-start | bytes 786440 | tf_op jit(solution)/shard_map/ppermute | solution.py:150
  228.9 15.1 %collective-permute-start.17 = (bf16[512,256]{1,0:T(8,128)(2,1)S(1)}, bf16[512,256]{1,0:T(8,128)(2,1)S(1)}, u32[]{:S(2)}, u32[]{:S(2)}) collective-permute-start(bf16[512,256]{1,0:T(8,128)(2,1)S(1)} %collective-permute-done.15.rl_ref), channel_id=1, source_target_pairs={{0,3},{1,0},{2,1},{3,2},{4,7},{5,4},{6,5},{7,6},{8,11},{9,8},{10,9... | collective-permute-start | bytes 786440 | tf_op jit(solution)/shard_map/ppermute | solution.py:150
  231.2 15.6 %all-to-all-start.4 = ((f32[8,16,256]{2,1,0:T(8,128)}), f32[8,16,256]{2,1,0:T(8,128)S(1)}, u32[]{:S(2)}, u32[]{:S(2)}) async-start(f32[8,16,256]{2,1,0:T(8,128)} %reduce_sum.18), calls=%async_computation.4 | async-start | bytes 262144 | tf_op jit(solution)/shard_map/all_to_all | solution.py:257
  (31 other events, 188.2 us)
Sparse Core Ops, SparseCore 0:
  121.5 43.3 all-gather.2

commit v2 on v0

v2 whole, which is shorter than its diff:
```python
import functools
import math

import jax
import jax.numpy as jnp
from jax import lax
from jax.experimental import pallas as pl
from jax.experimental.pallas import tpu as pltpu
from jax.sharding import Mesh
from jax.sharding import PartitionSpec as P

LAYERS = 3
BLK = 128
FEAT = 256
BATCH = 1024
HALF = 512
HALO = 3072
HIST = 2048
ROWS = 512
SLOTS = 12
RB = 8
HB = HALO // BLK
LATE = 10**11
TRAINER = ("z", "x", "core")

mixing = 0.1
strength = 0.5
bf16 = jnp.bfloat16
f32 = jnp.float32

VMEM = pl.BlockSpec(memory_space=pltpu.VMEM)
SMEM = pl.BlockSpec(memory_space=pltpu.SMEM)


def layer_share(layer_index):
    return math.log(strength / (layer_index + 1) + 1.0)


def call(kernel, name, flops, mib=24, **rest):
    return pl.pallas_call(
        kernel,
        name=name,
        compiler_params=pltpu.CompilerParams(vmem_limit_bytes=mib * 2**20),
        cost_estimate=pl.CostEstimate(flops=flops, bytes_accessed=4 << 20, transcendentals=0),
        **rest,
    )


def shape(*dims, dtype=bf16):
    return jax.ShapeDtypeStruct(dims, dtype)


def one_hot_of(ids):
    at = lax.broadcasted_iota(jnp.int32, (BLK, HIST), 1)
    parts = [(at == ids[:, b : b + 1]).astype(f32).astype(bf16) for b in range(ids.shape[1])]
    return jnp.concatenate(parts, 0)


def pick(chosen, rows):
    return jnp.dot(chosen, rows, preferred_element_type=f32).astype(bf16)


IDS = pl.BlockSpec((1, BLK, ROWS // BLK), lambda i: (i, 0, 0))


def send_first_kernel(ids_ref, rows_ref, out_ref):
    out_ref[...] = pick(one_hot_of(ids_ref[0]), rows_ref[...])


def send_first(ids, rows):
    return call(
        send_first_kernel,
        "send_first",
        2 * HALO * HIST * FEAT,
        grid=(HALO // ROWS,),
        in_specs=[IDS, pl.BlockSpec((HIST, FEAT), lambda i: (0, 0))],
        out_specs=pl.BlockSpec((ROWS, FEAT), lambda i: (i, 0)),
        out_shape=shape(HALO, FEAT),
    )(ids, rows)


def send_rest_kernel(ids_ref, zero_ref, one_ref, two_ref, send_one_ref, send_two_ref, start_ref):
    step = pl.program_id(0)
    chosen = one_hot_of(ids_ref[0])

    @pl.when(step >= 2)
    def _():
        send_one_ref[...] = pick(chosen, one_ref[0])
        send_two_ref[...] = pick(chosen, two_ref[0])

    @pl.when(step < 2)
    def _():
        start_ref[...] = pick(chosen, zero_ref[...])


def send_rest(ids, zero, history):
    late = lambda i: (jnp.maximum(i - 2, 0), 0)
    whole = lambda layer: pl.BlockSpec((1, HIST, FEAT), lambda i: (layer, 0, 0))
    return call(
        send_rest_kernel,
        "send_rest",
        2 * (2 * HALO + BATCH) * HIST * FEAT,
        grid=((HALO + BATCH) // ROWS,),
        in_specs=[IDS, pl.BlockSpec((HIST, FEAT), lambda i: (0, 0)), whole(1), whole(2)],
        out_specs=[
            pl.BlockSpec((ROWS, FEAT), late),
            pl.BlockSpec((ROWS, FEAT), late),
            pl.BlockSpec((ROWS, FEAT), lambda i: (jnp.minimum(i, 1), 0)),
        ],
        out_shape=[shape(HALO, FEAT), shape(HALO, FEAT), shape(BATCH, FEAT)],
    )(ids, zero, history, history)


def slab(w_ref, me, by):
    at = lax.rem(me + by, 4) * FEAT
    return w_ref[0, pl.ds(pl.multiple_of(at, FEAT), FEAT), :]


def mixed(share, me, w_ref, refs):
    own = refs[0][...]
    total = jnp.zeros(own.shape, f32)
    for ref, by in zip(refs, (0, 3, 1, 2)):
        total += jnp.dot(ref[...], slab(w_ref, me, by), preferred_element_type=f32)
    return (1.0 - share) * own.astype(f32) + share * total


def product(r, cols_ref, count_ref, adj_ref, x_ref):
    total = jnp.zeros((BLK, FEAT), f32)
    count = count_ref[r]
    for k in range(0, SLOTS, 2):
        left, right = [], []
        for slot in (k, k + 1):
            block = adj_ref[r, slot]
            left.append(jnp.where(slot < count, block, jnp.zeros_like(block)))
            right.append(x_ref[cols_ref[r, slot]])
        total += jnp.dot(jnp.concatenate(left, 1), jnp.concatenate(right, 0), preferred_element_type=f32)
    return total


def block(r):
    return pl.ds(r * BLK, BLK)


def put(up_ref, low_ref, r, value):
    ref = up_ref if r < RB // 2 else low_ref
    ref[block(r % (RB // 2)), :] = value


def supported(total, start_ref, r):
    return ((1.0 - mixing) * total + mixing * start_ref[block(r), :].astype(f32)).astype(bf16)


def layer_kernel(cols_ref, count_ref, up_ref, low_ref, halo_ref, start_ref, adj_ref, out_up_ref, out_low_ref, x_ref):
    x_ref[: RB // 2] = up_ref[...].reshape(RB // 2, BLK, FEAT)
    x_ref[RB // 2 : RB] = low_ref[...].reshape(RB // 2, BLK, FEAT)
    x_ref[RB:] = halo_ref[...].reshape(HB, BLK, FEAT)
    for r in range(RB):
        put(out_up_ref, out_low_ref, r, supported(product(r, cols_ref, count_ref, adj_ref, x_ref), start_ref, r))


def layer(cols, count, rows, halo, start, adjacency):
    return call(
        layer_kernel,
        "layer",
        2 * BATCH * SLOTS * BLK * FEAT,
        in_specs=[SMEM, SMEM] + [VMEM] * 5,
        out_specs=[VMEM, VMEM],
        out_shape=[shape(HALF, FEAT)] * 2,
        scratch_shapes=[pltpu.VMEM((RB + HB, BLK, FEAT), bf16)],
    )(cols, count, *rows, halo, start, adjacency)


def mix_kernel(share, me_ref, up_ref, low_ref, lu_ref, ll_ref, ru_ref, rl_ref, fu_ref, fl_ref, w_ref, out_up_ref, out_low_ref):
    me = me_ref[0]
    out_up_ref[...] = jnp.maximum(mixed(share, me, w_ref, (up_ref, lu_ref, ru_ref, fu_ref)), 0.0).astype(bf16)
    out_low_ref[...] = jnp.maximum(mixed(share, me, w_ref, (low_ref, ll_ref, rl_ref, fl_ref)), 0.0).astype(bf16)


def mix(index, me, rows, others, weights):
    half = pl.BlockSpec((HALF, FEAT), lambda i: (0, 0))
    return call(
        functools.partial(mix_kernel, layer_share(index)),
        "mix",
        2 * BATCH * 4 * FEAT * FEAT,
        grid=(1,),
        in_specs=[SMEM] + [half] * 8 + [pl.BlockSpec((1, 4 * FEAT, FEAT), lambda i: (index, 0, 0))],
        out_specs=[half, half],
        out_shape=[shape(HALF, FEAT)] * 2,
    )(me, *rows, *others, weights)


def mix_last_kernel(me_ref, up_ref, low_ref, lu_ref, ll_ref, ru_ref, rl_ref, fu_ref, fl_ref, w_ref, out_ref):
    me, share = me_ref[0], layer_share(2)
    out_ref[:HALF] = mixed(share, me, w_ref, (up_ref, lu_ref, ru_ref, fu_ref)).astype(bf16)
    out_ref[HALF:] = mixed(share, me, w_ref, (low_ref, ll_ref, rl_ref, fl_ref)).astype(bf16)


def mix_last(me, rows, others, weights):
    half = pl.BlockSpec((HALF, FEAT), lambda i: (0, 0))
    return call(
        mix_last_kernel,
        "mix_last",
        LATE,
        grid=(1,),
        in_specs=[SMEM] + [half] * 8 + [pl.BlockSpec((1, 4 * FEAT, FEAT), lambda i: (2, 0, 0))],
        out_specs=pl.BlockSpec((BATCH, FEAT), lambda i: (0, 0)),
        out_shape=shape(BATCH, FEAT),
    )(me, *rows, *others, weights)


def write_kernel(ids_ref, history_ref, *refs):
    base = pl.program_id(0) * ROWS
    at = lax.broadcasted_iota(jnp.int32, (ROWS, BATCH), 0) + base
    chosen = (at == ids_ref[...]).astype(f32)
    hit = jnp.max(chosen, axis=1, keepdims=True) > 0.0
    rows = jnp.concatenate([refs[0][...], refs[1][...]], 0)
    refs[-1][0] = jnp.where(hit, pick(chosen.astype(bf16), rows), history_ref[0])


def write_rows(layer, ids, history, rows, so_far=None):
    in_specs = [
        pl.BlockSpec((1, BATCH), lambda i: (0, 0)),
        pl.BlockSpec((1, ROWS, FEAT), lambda i: (layer + 1, i, 0)),
    ] + [pl.BlockSpec(part.shape, lambda i: (0, 0)) for part in rows]
    if so_far is not None:
        in_specs.append(pl.BlockSpec(memory_space=pl.ANY))
    return call(
        write_kernel,
        "write_rows",
        2 * BATCH * HIST * FEAT,
        grid=(HIST // ROWS,),
        in_specs=in_specs,
        out_specs=pl.BlockSpec((1, ROWS, FEAT), lambda i: (layer, i, 0)),
        out_shape=shape(2, HIST, FEAT),
        input_output_aliases={} if so_far is None else {len(in_specs) - 1: 0},
    )(ids, history, *rows, *(() if so_far is None else (so_far,)))


def grad_kernel(core_ref, me_ref, up_ref, low_ref, own_ref, left_ref, right_ref, far_ref, keep_ref, send_ref, acc_ref):
    support = jnp.concatenate([up_ref[...], low_ref[...]], 0)
    for by, ref in ((0, own_ref), (3, left_ref), (1, right_ref), (2, far_ref)):
        term = lax.dot_general(support, ref[...], (((0,), (0,)), ((), ())), preferred_element_type=f32)
        acc_ref[lax.rem(me_ref[0] + by, 4)] = term.reshape(8, 32, FEAT)
    mine = pl.multiple_of(core_ref[0] * 16, 16)
    theirs = pl.multiple_of(16 - core_ref[0] * 16, 16)
    for low in range(2):
        for x in range(4):
            group = low * 4 + x
            for y in range(4):
                keep_ref[x * 4 + y, low] = acc_ref[y, group, pl.ds(mine, 16), :]
                send_ref[x * 4 + y, low] = acc_ref[y, group, pl.ds(theirs, 16), :]


def grad_terms(core, me, support, own, parts):
    return call(
        grad_kernel,
        "grad_terms",
        2 * BATCH * FEAT * 4 * FEAT,
        in_specs=[SMEM, SMEM] + [VMEM] * 6,
        out_specs=[VMEM, VMEM],
        out_shape=[shape(16, 2, 16, FEAT, dtype=f32)] * 2,
        scratch_shapes=[pltpu.VMEM((4, 8, 32, FEAT), f32)],
    )(core, me, *support, own, *parts)


def shift(array, axis, size, by):
    return lax.ppermute(array, axis, [(i, (i + by) % size) for i in range(size)])


def ring_gather(up, low):
    left_up, right_low = shift(up, "y", 4, 1), shift(low, "y", 4, 3)
    left_low, right_up = shift(low, "y", 4, 1), shift(up, "y", 4, 3)
    far_up, far_low = shift(left_up, "y", 4, 1), shift(right_low, "y", 4, 3)
    return left_up, left_low, right_up, right_low, far_up, far_low


def halves(rows):
    return rows[: rows.shape[0] // 2], rows[rows.shape[0] // 2 :]


def after(value, *others):
    return lax.optimization_barrier((value, *others))[0]


def reduce_grad(keep, send):
    total = (keep + shift(send, "core", 2, 1)).astype(bf16).reshape(16, 32, FEAT)
    total = lax.all_to_all(total, ("x", "y"), 0, 0, tiled=True)
    total = total.reshape(4, 8, 16, FEAT).astype(f32).sum(0)
    across = lax.all_to_all(total, "z", 0, 0, tiled=True)
    return across.sum(0) * layer_share(LAYERS - 1)


def body(history, send_rows, batch_ids, block_cols, block_count, adjacency, weights, cotangent):
    me = lax.axis_index("y").astype(jnp.int32).reshape(1)
    core = lax.axis_index("core").astype(jnp.int32).reshape(1)
    by_step = lambda ids: ids.reshape(-1, ROWS // BLK, BLK).transpose(0, 2, 1)
    send_ids = by_step(send_rows)

    def exchange(rows):
        rows = rows.reshape(64, HALO // 64, FEAT)
        return lax.all_to_all(rows, TRAINER, 0, 0, tiled=True).reshape(HALO, FEAT)

    zero = history[0]
    sent = send_first(send_ids, zero)
    halo = exchange(sent)
    own_cot = after(cotangent, sent)
    others_cot = tuple(shift(own_cot, "y", 4, by) for by in (1, 3, 2))
    send_one, send_two, start = send_rest(jnp.concatenate([by_step(batch_ids), send_ids], 0), zero, history)
    halo_one = exchange(after(send_one, *others_cot))

    support = layer(block_cols, block_count, halves(start), halo, start, adjacency)
    one = mix(0, me, support, ring_gather(*support), weights)
    halo_two = exchange(after(send_two, *one))
    fresh = write_rows(0, batch_ids, history, one)
    support = layer(block_cols, block_count, one, halo_one, start, adjacency)
    two = mix(1, me, support, ring_gather(*support), weights)
    fresh = write_rows(1, batch_ids, history, two, fresh)
    support = layer(block_cols, block_count, after(tuple(two), fresh), halo_two, start, adjacency)
    others = ring_gather(*support)
    grad = reduce_grad(*grad_terms(core, me, support, cotangent, others_cot))
    final = mix_last(me, support, others, weights)
    return fresh, final, grad


def solution(mesh):
    fine = Mesh(mesh.devices.reshape(8, 4, 2, 4), ("z", "x", "core", "y"))
    return jax.shard_map(
        body,
        mesh=fine,
        in_specs=(
            P(None, TRAINER, "y"),
            P(TRAINER, None, None),
            P(TRAINER, None),
            P(TRAINER, None),
            P(TRAINER),
            P(TRAINER, None, None, None),
            P(None, None, "y"),
            P(TRAINER, "y"),
        ),
        out_specs=(P(None, TRAINER, "y"), P(TRAINER, "y"), P(TRAINER, "y")),
        check_vma=False,
    )
```

time: 429 us -> 194 us (0.45)
  waiting for transfers between devices: 266 us -> 64.7 us
  local copies, waits for them, and re-layouts: 83.1 us -> 22.1 us
  Pallas kernels: 0 us -> 43.3 us
  starting transfers between devices: 23.8 us -> 57.6 us
  matrix products: 26.9 us -> 0 us
  between operations: 14 us -> 0.91 us
  other arithmetic: 14.5 us -> 3.02 us
    reduce_scatter x1 -> x0, waiting for transfers between devices: 125 us -> none  [body(): lax.psum_scatter(totals[1], 'trainer', scatter_dimension=0, tiled=True)]
    gather x7 -> x0, local copies, waits for them, and re-layouts: 67.3 us -> none  [the longest x3 39.7 us: body(): history[layer_index][send_rows[0]]]
    all_gather x3 -> x0, waiting for transfers between devices: 60.8 us -> none  [fold_columns(): return add_columns(lax.all_gather(support, 'mp', axis=1, tiled=True))]
    all_to_all x3 -> x5, waiting for transfers between devices: 79.8 us -> 33.2 us  [the longest x3 28.8 us: exchange(): return lax.all_to_all(rows, TRAINER, 0, 0, tiled=True).reshape(HALO, FEAT)]
    pallas_call x0 -> x11, Pallas kernels: none -> 43.3 us  [the longest x1 13.5 us: send_rest(): call(send_rest_kernel, 'send_rest', 2 * (2 * HALO + BATCH) * HIST * FEAT,...]
    ppermute x0 -> x22, waiting for transfers between devices: none -> 31.6 us  [shift(): lax.ppermute(array, axis, [(i, (i + by) % size) for i in range(size)])]
    dot_general x7 -> x0, matrix products: 26.9 us -> none  [the longest x3 14.4 us: aggregate_blocks(): jnp.einsum('rkij,rkjd->rid', masked, picked, preferred_element_type=jnp.f...]
    ppermute x0 -> x22, starting transfers between devices: none -> 23 us  [shift(): lax.ppermute(array, axis, [(i, (i + by) % size) for i in range(size)])]
  transfers between devices with their start and end apart: 7 -> 27, of which waited for: 7 -> 17; matrix products, arithmetic and copies ran while one was open for 12% -> 2% of each run, Pallas kernels for 0% -> 17%
where the time goes in v2:
time: 194 us; the launch traced here: 192 us
  waiting for transfers between devices  64.7 us (33%)
  starting transfers between devices  57.6 us (30%)
  Pallas kernels  43.3 us (22%)
  local copies, waits for them, and re-layouts  22.1 us (11%)
  other arithmetic  3.02 us (2%)
    ppermute x22, waiting for transfers between devices, shift(): lax.ppermute(array, axis, [(i, (i + by) % size) for i in range(size)])  31.6 us
    all_to_all x3, waiting for transfers between devices, exchange(): return lax.all_to_all(rows, TRAINER, 0, 0, tiled=True).reshape(HALO, FEAT)  28.8 us
    all_to_all x3, starting transfers between devices, exchange(): return lax.all_to_all(rows, TRAINER, 0, 0, tiled=True).reshape(HALO, FEAT)  23.8 us
    ppermute x22, starting transfers between devices, shift(): lax.ppermute(array, axis, [(i, (i + by) % size) for i in range(size)])  23 us
    unnamed x55, local copies, waits for them, and re-layouts  18.6 us
    pallas_call x1, Pallas kernels, send_rest(): call(send_rest_kernel, 'send_rest', 2 * (2 * HALO + BATCH) * HIST * FEAT,...  13.5 us
    pallas_call x3, Pallas kernels, layer(): call(layer_kernel, 'layer', 2 * BATCH * SLOTS * BLK * FEAT, in_specs=[SME...  10.1 us
    all_to_all x1, starting transfers between devices, reduce_grad(): total = lax.all_to_all(total, ('x', 'y'), 0, 0, tiled=True)  7.36 us
  transfers between devices with their start and end apart: 27, of which 17 were waited for; matrix products, arithmetic and copies ran while one was open for 2% of the time, Pallas kernels for 17%

profile of v2, /device:TPU:8, one launch (start us, length us, event | category | flops | bytes accessed | tf_op | source)
XLA Modules:
  0.0 191.7 jit_solution(17935534444677088384)
XLA Ops:
  3.1 4.6 %send_first.1 = bf16[3072,256]{1,0:T(8,128)(2,1)S(1)} custom-call(s32[6,128,4]{2,1,0:T(8,128)S(1)} %bitcast.19, bf16[2048,256]{1,0:T(8,128)(2,1)S(1)} %slice_bitcast_fusion.zero_ref.rows_ref), custom_call_target="tpu_custom_call" | custom-call | flops 3221225472 | bytes 4194304 | tf_op jit(solution)/shard_map/send_first/pallas_call | solution.py:71
  8.8 12.4 %all-to-all-start = ((bf16[64,48,256]{2,1,0:T(8,128)(2,1)}), bf16[64,48,256]{2,1,0:T(8,128)(2,1)}, u32[]{:S(2)}, u32[]{:S(2)}) async-start(bf16[64,48,256]{2,1,0:T(8,128)(2,1)} %bitcast.18), calls=%async_computation | async-start | bytes 3145728 | tf_op jit(solution)/shard_map/all_to_all | solution.py:301
  28.6 13.5 %send_rest.1 = (bf16[3072,256]{1,0:T(8,128)(2,1)S(1)}, bf16[3072,256]{1,0:T(8,128)(2,1)S(1)}, bf16[1024,256]{1,0:T(8,128)(2,1)S(1)}) custom-call(s32[8,128,4]{2,1,0:T(8,128)S(1)} %pad_add_fusion.ids_ref, bf16[2048,256]{1,0:T(8,128)(2,1)S(1)} %copy-done.15, bf16[3,2048,256]{2,1,0:T(8,128)(2,1)S(1)} %copy-done.1, bf16[3,2048,256]{2,1,0:T(8,128)(2,1)S(1)} %copy-done.1), custom_call_target="tpu_custom_call" | custom-call | flops 7516192768 | bytes 4194304 | tf_op jit(solution)/shard_map/send_rest/pallas_call | solution.py:99
  45.2 3.0 %collective-permute-done.7.right_ref = bf16[1024,256]{1,0:T(8,128)(2,1)} collective-permute-done((bf16[1024,256]{1,0:T(8,128)(2,1)}, bf16[1024,256]{1,0:T(8,128)(2,1)}, u32[]{:S(2)}, u32[]{:S(2)}) %collective-permute-start.7) | collective-permute-done | bytes 524320 | tf_op jit(solution)/shard_map/ppermute | solution.py:267
  48.4 12.9 %all-to-all-done = bf16[64,48,256]{2,1,0:T(8,128)(2,1)} async-done(((bf16[64,48,256]{2,1,0:T(8,128)(2,1)}), bf16[64,48,256]{2,1,0:T(8,128)(2,1)}, u32[]{:S(2)}, u32[]{:S(2)}) %all-to-all-start) | async-done | bytes 1572896 | tf_op jit(solution)/shard_map/all_to_all | solution.py:301
  61.2 5.8 %all-to-all-start.1 = ((bf16[64,48,256]{2,1,0:T(8,128)(2,1)}), bf16[64,48,256]{2,1,0:T(8,128)(2,1)}, u32[]{:S(2)}, u32[]{:S(2)}) async-start(bf16[64,48,256]{2,1,0:T(8,128)(2,1)} %bitcast.17), calls=%async_computation.1 | async-start | bytes 3145728 | tf_op jit(solution)/shard_map/all_to_all | solution.py:301
  69.2 3.3 %layer.3 = (bf16[512,256]{1,0:T(8,128)(2,1)S(1)}, bf16[512,256]{1,0:T(8,128)(2,1)}) custom-call(s32[8,12]{1,0:T(8,128)S(1)} %copy-done.25, s32[8]{0:T(128)S(1)} %copy-done.26, bf16[512,256]{1,0:T(8,128)(2,1)S(1)} %get-tuple-element.44.up_ref, bf16[512,256]{1,0:T(8,128)(2,1)S(1)} %get-tuple-element.43.low_ref, bf16[3072,256]{1,0:T(8,128)(2,1)} %bitcast.6.halo_ref, ...), custom_call_target="tpu_custom_call" | custom-call | flops 805306368 | bytes 4194304 | tf_op jit(solution)/shard_map/layer/pallas_call | solution.py:162
  77.4 4.5 %collective-permute-done.lu_ref = bf16[512,256]{1,0:T(8,128)(2,1)} collective-permute-done((bf16[512,256]{1,0:T(8,128)(2,1)S(1)}, bf16[512,256]{1,0:T(8,128)(2,1)}, u32[]{:S(2)}, u32[]{:S(2)}) %collective-permute-start) | collective-permute-done | bytes 262176 | tf_op jit(solution)/shard_map/ppermute | solution.py:267
  84.1 5.2 %collective-permute-done.2.ru_ref = bf16[512,256]{1,0:T(8,128)(2,1)} collective-permute-done((bf16[512,256]{1,0:T(8,128)(2,1)S(1)}, bf16[512,256]{1,0:T(8,128)(2,1)}, u32[]{:S(2)}, u32[]{:S(2)}) %collective-permute-start.2) | collective-permute-done | bytes 262176 | tf_op jit(solution)/shard_map/ppermute | solution.py:267
  89.3 2.8 %collective-permute-done.4.fu_ref = bf16[512,256]{1,0:T(8,128)(2,1)} collective-permute-done((bf16[512,256]{1,0:T(8,128)(2,1)}, bf16[512,256]{1,0:T(8,128)(2,1)}, u32[]{:S(2)}, u32[]{:S(2)}) %collective-permute-start.4) | collective-permute-done | bytes 262176 | tf_op jit(solution)/shard_map/ppermute | solution.py:267
  98.9 8.2 %all-to-all-done.1 = bf16[64,48,256]{2,1,0:T(8,128)(2,1)} async-done(((bf16[64,48,256]{2,1,0:T(8,128)(2,1)}), bf16[64,48,256]{2,1,0:T(8,128)(2,1)}, u32[]{:S(2)}, u32[]{:S(2)}) %all-to-all-start.1) | async-done | bytes 1572896 | tf_op jit(solution)/shard_map/all_to_all | solution.py:301
  107.1 5.6 %all-to-all-start.2 = ((bf16[64,48,256]{2,1,0:T(8,128)(2,1)}), bf16[64,48,256]{2,1,0:T(8,128)(2,1)}, u32[]{:S(2)}, u32[]{:S(2)}) async-start(bf16[64,48,256]{2,1,0:T(8,128)(2,1)} %bitcast.16), calls=%async_computation.2 | async-start | bytes 3145728 | tf_op jit(solution)/shard_map/all_to_all | solution.py:301
  114.6 3.4 %layer.4 = (bf16[512,256]{1,0:T(8,128)(2,1)}, bf16[512,256]{1,0:T(8,128)(2,1)}) custom-call(s32[8,12]{1,0:T(8,128)S(1)} %copy-done.25, s32[8]{0:T(128)S(1)} %copy-done.26, bf16[512,256]{1,0:T(8,128)(2,1)S(1)} %get-tuple-element.26.up_ref.refs_0_, bf16[512,256]{1,0:T(8,128)(2,1)S(1)} %copy-done.17, bf16[3072,256]{1,0:T(8,128)(2,1)} %bitcast.8.halo_ref, ...), custom_call_target="tpu_custom_call" | custom-call | flops 805306368 | bytes 4194304 | tf_op jit(solution)/shard_map/layer/pallas_call | solution.py:162
  122.1 5.4 %collective-permute-done.9.lu_ref = bf16[512,256]{1,0:T(8,128)(2,1)} collective-permute-done((bf16[512,256]{1,0:T(8,128)(2,1)}, bf16[512,256]{1,0:T(8,128)(2,1)}, u32[]{:S(2)}, u32[]{:S(2)}) %collective-permute-start.9) | collective-permute-done | bytes 262176 | tf_op jit(solution)/shard_map/ppermute | solution.py:267
  132.4 2.9 %write_rows.2.refs_2_ = bf16[2,2048,256]{2,1,0:T(8,128)(2,1)} custom-call(s32[1,1024]{1,0:T(1,128)S(1)} %copy-done.24, bf16[3,2048,256]{2,1,0:T(8,128)(2,1)S(1)} %copy-done.2, bf16[512,256]{1,0:T(8,128)(2,1)S(1)} %get-tuple-element.26.up_ref.refs_0_, bf16[512,256]{1,0:T(8,128)(2,1)S(1)} %copy-done.18), custom_call_target="tpu_custom_call" | custom-call | flops 1073741824 | bytes 4194304 | tf_op jit(solution)/shard_map/write_rows/pallas_call | solution.py:227
  135.4 2.4 %collective-permute-done.13.fu_ref = bf16[512,256]{1,0:T(8,128)(2,1)} collective-permute-done((bf16[512,256]{1,0:T(8,128)(2,1)}, bf16[512,256]{1,0:T(8,128)(2,1)}, u32[]{:S(2)}, u32[]{:S(2)}) %collective-permute-start.13) | collective-permute-done | bytes 262176 | tf_op jit(solution)/shard_map/ppermute | solution.py:267
  141.3 3.0 %write_rows.3 = bf16[2,2048,256]{2,1,0:T(8,128)(2,1)} custom-call(s32[1,1024]{1,0:T(1,128)S(1)} %copy-done.24, bf16[3,2048,256]{2,1,0:T(8,128)(2,1)S(1)} %copy-done.3, bf16[512,256]{1,0:T(8,128)(2,1)S(1)} %get-tuple-element.35.refs_0_.up_ref, bf16[512,256]{1,0:T(8,128)(2,1)S(1)} %get-tuple-element.36.refs_1_.low_ref, ...), custom_call_target="tpu_custom_call", output_to_operand_aliasing={{}: (4, {})} | custom-call | flops 1073741824 | bytes 4194304 | tf_op jit(solution)/shard_map/write_rows/pallas_call | solution.py:227
  145.0 7.7 %all-to-all-done.2 = bf16[64,48,256]{2,1,0:T(8,128)(2,1)} async-done(((bf16[64,48,256]{2,1,0:T(8,128)(2,1)}), bf16[64,48,256]{2,1,0:T(8,128)(2,1)}, u32[]{:S(2)}, u32[]{:S(2)}) %all-to-all-start.2) | async-done | bytes 1572896 | tf_op jit(solution)/shard_map/all_to_all | solution.py:301
  154.6 3.4 %layer.5 = (bf16[512,256]{1,0:T(8,128)(2,1)}, bf16[512,256]{1,0:T(8,128)(2,1)}) custom-call(s32[8,12]{1,0:T(8,128)S(1)} %copy-done.25, s32[8]{0:T(128)S(1)} %copy-done.26, bf16[512,256]{1,0:T(8,128)(2,1)S(1)} %get-tuple-element.35.refs_0_.up_ref, bf16[512,256]{1,0:T(8,128)(2,1)S(1)} %copy-done.20, bf16[3072,256]{1,0:T(8,128)(2,1)} %bitcast.10.halo_ref, ...), custom_call_target="tpu_custom_call" | custom-call | flops 805306368 | bytes 4194304 | tf_op jit(solution)/shard_map/layer/pallas_call | solution.py:162
  163.6 7.4 %all-to-all-start.3 = ((bf16[16,32,256]{2,1,0:T(8,128)(2,1)}), bf16[16,32,256]{2,1,0:T(8,128)(2,1)S(1)}, u32[]{:S(2)}, u32[]{:S(2)}) async-start(bf16[16,32,256]{2,1,0:T(8,128)(2,1)} %bitcast.12), calls=%async_computation.3 | async-start | bytes 524288 | tf_op jit(solution)/shard_map/all_to_all | solution.py:287
  175.1 2.9 %all-to-all-done.3 = bf16[16,32,256]{2,1,0:T(8,128)(2,1)S(1)} async-done(((bf16[16,32,256]{2,1,0:T(8,128)(2,1)}), bf16[16,32,256]{2,1,0:T(8,128)(2,1)S(1)}, u32[]{:S(2)}, u32[]{:S(2)}) %all-to-all-start.3) | async-done | bytes 262176 | tf_op jit(solution)/shard_map/all_to_all | solution.py:287
  178.7 3.4 %all-to-all-start.4 = ((f32[8,16,256]{2,1,0:T(8,128)}), f32[8,16,256]{2,1,0:T(8,128)S(1)}, u32[]{:S(2)}, u32[]{:S(2)}) async-start(f32[8,16,256]{2,1,0:T(8,128)} %convert_reduce_fusion), calls=%async_computation.4 | async-start | bytes 262144 | tf_op jit(solution)/shard_map/all_to_all | solution.py:289
  182.6 4.5 %collective-permute-done.19.fu_ref = bf16[512,256]{1,0:T(8,128)(2,1)S(1)} collective-permute-done((bf16[512,256]{1,0:T(8,128)(2,1)S(1)}, bf16[512,256]{1,0:T(8,128)(2,1)S(1)}, u32[]{:S(2)}, u32[]{:S(2)}) %collective-permute-start.19) | collective-permute-done | bytes 262176 | tf_op jit(solution)/shard_map/ppermute | solution.py:267
  187.0 2.5 %mix_last.1 = bf16[1024,256]{1,0:T(8,128)(2,1)} custom-call(s32[1]{0:T(128)} %bitcast.me_ref, bf16[512,256]{1,0:T(8,128)(2,1)} %get-tuple-element.39.up_ref, bf16[512,256]{1,0:T(8,128)(2,1)} %get-tuple-element.40.low_ref, bf16[512,256]{1,0:T(8,128)(2,1)S(1)} %collective-permute-done.15.lu_ref, bf16[512,256]{1,0:T(8,128)(2,1)S(1)} %collective-permute-done.16.ll_ref, ...), custom_call_target="tpu_custom_call" | custom-call | flops 99999997952 | bytes 4194304 | tf_op jit(solution)/shard_map/mix_last/pallas_call | solution.py:200
  (106 shorter events, 60.1 us)
Async XLA Ops:
  8.8 52.4 %all-to-all-start = ((bf16[64,48,256]{2,1,0:T(8,128)(2,1)}), bf16[64,48,256]{2,1,0:T(8,128)(2,1)}, u32[]{:S(2)}, u32[]{:S(2)}) async-start(bf16[64,48,256]{2,1,0:T(8,128)(2,1)} %bitcast.18), calls=%async_computation | async-start | bytes 3145728 | tf_op jit(solution)/shard_map/all_to_all | solution.py:301
  21.2 24.0 %collective-permute-start.8 = (bf16[1024,256]{1,0:T(8,128)(2,1)}, bf16[1024,256]{1,0:T(8,128)(2,1)}, u32[]{:S(2)}, u32[]{:S(2)}) collective-permute-start(bf16[1024,256]{1,0:T(8,128)(2,1)} %own_ref.1), channel_id=1, source_target_pairs={{0,2},{1,3},{2,0},{3,1},{4,6},{5,7},{6,4},{7,5},{8,10},{9,11},{10,... | collective-permute-start | bytes 1572872 | tf_op jit(solution)/shard_map/ppermute | solution.py:267
  23.6 24.6 %collective-permute-start.7 = (bf16[1024,256]{1,0:T(8,128)(2,1)}, bf16[1024,256]{1,0:T(8,128)(2,1)}, u32[]{:S(2)}, u32[]{:S(2)}) collective-permute-start(bf16[1024,256]{1,0:T(8,128)(2,1)} %own_ref.1), channel_id=1, source_target_pairs={{0,3},{1,0},{2,1},{3,2},{4,7},{5,4},{6,5},{7,6},{8,11},{9,8},{10,9... | collective-permute-start | bytes 1572872 | tf_op jit(solution)/shard_map/ppermute | solution.py:267
  25.0 23.4 %collective-permute-start.6 = (bf16[1024,256]{1,0:T(8,128)(2,1)}, bf16[1024,256]{1,0:T(8,128)(2,1)}, u32[]{:S(2)}, u32[]{:S(2)}) collective-permute-start(bf16[1024,256]{1,0:T(8,128)(2,1)} %own_ref.1), channel_id=1, source_target_pairs={{0,1},{1,2},{2,3},{3,0},{4,5},{5,6},{6,7},{7,4},{8,9},{9,10},{10,1... | collective-permute-start | bytes 1572872 | tf_op jit(solution)/shard_map/ppermute | solution.py:267
  61.2 45.8 %all-to-all-start.1 = ((bf16[64,48,256]{2,1,0:T(8,128)(2,1)}), bf16[64,48,256]{2,1,0:T(8,128)(2,1)}, u32[]{:S(2)}, u32[]{:S(2)}) async-start(bf16[64,48,256]{2,1,0:T(8,128)(2,1)} %bitcast.17), calls=%async_computation.1 | async-start | bytes 3145728 | tf_op jit(solution)/shard_map/all_to_all | solution.py:301
  74.2 9.5 %collective-permute-start.3 = (bf16[512,256]{1,0:T(8,128)(2,1)}, bf16[512,256]{1,0:T(8,128)(2,1)}, u32[]{:S(2)}, u32[]{:S(2)}) collective-permute-start(bf16[512,256]{1,0:T(8,128)(2,1)} %get-tuple-element.25.low_ref), channel_id=1, source_target_pairs={{0,3},{1,0},{2,1},{3,2},{4,7},{5,4},{6,5},{7,6},{8,11},{9,8},{10,9... | collective-permute-start | bytes 786440 | tf_op jit(solution)/shard_map/ppermute | solution.py:267
  74.6 14.7 %collective-permute-start.2 = (bf16[512,256]{1,0:T(8,128)(2,1)S(1)}, bf16[512,256]{1,0:T(8,128)(2,1)}, u32[]{:S(2)}, u32[]{:S(2)}) collective-permute-start(bf16[512,256]{1,0:T(8,128)(2,1)S(1)} %get-tuple-element.24.up_ref), channel_id=1, source_target_pairs={{0,3},{1,0},{2,1},{3,2},{4,7},{5,4},{6,5},{7,6},{8,11},{9,8},{10,9... | collective-permute-start | bytes 786440 | tf_op jit(solution)/shard_map/ppermute | solution.py:267
  77.0 12.3 %collective-permute-start.1 = (bf16[512,256]{1,0:T(8,128)(2,1)}, bf16[512,256]{1,0:T(8,128)(2,1)}, u32[]{:S(2)}, u32[]{:S(2)}) collective-permute-start(bf16[512,256]{1,0:T(8,128)(2,1)} %get-tuple-element.25.low_ref), channel_id=1, source_target_pairs={{0,1},{1,2},{2,3},{3,0},{4,5},{5,6},{6,7},{7,4},{8,9},{9,10},{10,1... | collective-permute-start | bytes 786440 | tf_op jit(solution)/shard_map/ppermute | solution.py:267
  81.9 10.3 %collective-permute-start.4 = (bf16[512,256]{1,0:T(8,128)(2,1)}, bf16[512,256]{1,0:T(8,128)(2,1)}, u32[]{:S(2)}, u32[]{:S(2)}) collective-permute-start(bf16[512,256]{1,0:T(8,128)(2,1)} %collective-permute-done.lu_ref), channel_id=1, source_target_pairs={{0,1},{1,2},{2,3},{3,0},{4,5},{5,6},{6,7},{7,4},{8,9},{9,10},{10,1... | collective-permute-start | bytes 786440 | tf_op jit(solution)/shard_map/ppermute | solution.py:267
  83.7 9.9 %collective-permute-start.5 = (bf16[512,256]{1,0:T(8,128)(2,1)}, bf16[512,256]{1,0:T(8,128)(2,1)}, u32[]{:S(2)}, u32[]{:S(2)}) collective-permute-start(bf16[512,256]{1,0:T(8,128)(2,1)} %collective-permute-done.3.rl_ref), channel_id=1, source_target_pairs={{0,3},{1,0},{2,1},{3,2},{4,7},{5,4},{6,5},{7,6},{8,11},{9,8},{10,9... | collective-permute-start | bytes 786440 | tf_op jit(solution)/shard_map/ppermute | solution.py:267
  107.1 45.6 %all-to-all-start.2 = ((bf16[64,48,256]{2,1,0:T(8,128)(2,1)}), bf16[64,48,256]{2,1,0:T(8,128)(2,1)}, u32[]{:S(2)}, u32[]{:S(2)}) async-start(bf16[64,48,256]{2,1,0:T(8,128)(2,1)} %bitcast.16), calls=%async_computation.2 | async-start | bytes 3145728 | tf_op jit(solution)/shard_map/all_to_all | solution.py:301
  119.6 9.5 %collective-permute-start.12 = (bf16[512,256]{1,0:T(8,128)(2,1)}, bf16[512,256]{1,0:T(8,128)(2,1)}, u32[]{:S(2)}, u32[]{:S(2)}) collective-permute-start(bf16[512,256]{1,0:T(8,128)(2,1)} %get-tuple-element.32.low_ref), channel_id=1, source_target_pairs={{0,3},{1,0},{2,1},{3,2},{4,7},{5,4},{6,5},{7,6},{8,11},{9,8},{10,9... | collective-permute-start | bytes 786440 | tf_op jit(solution)/shard_map/ppermute | solution.py:267
  120.0 15.3 %collective-permute-start.11 = (bf16[512,256]{1,0:T(8,128)(2,1)}, bf16[512,256]{1,0:T(8,128)(2,1)}, u32[]{:S(2)}, u32[]{:S(2)}) collective-permute-start(bf16[512,256]{1,0:T(8,128)(2,1)} %get-tuple-element.31.up_ref), channel_id=1, source_target_pairs={{0,3},{1,0},{2,1},{3,2},{4,7},{5,4},{6,5},{7,6},{8,11},{9,8},{10,9... | collective-permute-start | bytes 786440 | tf_op jit(solution)/shard_map/ppermute | solution.py:267
  121.7 13.6 %collective-permute-start.10 = (bf16[512,256]{1,0:T(8,128)(2,1)}, bf16[512,256]{1,0:T(8,128)(2,1)}, u32[]{:S(2)}, u32[]{:S(2)}) collective-permute-start(bf16[512,256]{1,0:T(8,128)(2,1)} %get-tuple-element.32.low_ref), channel_id=1, source_target_pairs={{0,1},{1,2},{2,3},{3,0},{4,5},{5,6},{6,7},{7,4},{8,9},{9,10},{10,1... | collective-permute-start | bytes 786440 | tf_op jit(solution)/shard_map/ppermute | solution.py:267
  127.5 10.3 %collective-permute-start.13 = (bf16[512,256]{1,0:T(8,128)(2,1)}, bf16[512,256]{1,0:T(8,128)(2,1)}, u32[]{:S(2)}, u32[]{:S(2)}) collective-permute-start(bf16[512,256]{1,0:T(8,128)(2,1)} %collective-permute-done.9.lu_ref), channel_id=1, source_target_pairs={{0,1},{1,2},{2,3},{3,0},{4,5},{5,6},{6,7},{7,4},{8,9},{9,10},{10,1... | collective-permute-start | bytes 786440 | tf_op jit(solution)/shard_map/ppermute | solution.py:267
  129.1 9.9 %collective-permute-start.14 = (bf16[512,256]{1,0:T(8,128)(2,1)}, bf16[512,256]{1,0:T(8,128)(2,1)}, u32[]{:S(2)}, u32[]{:S(2)}) collective-permute-start(bf16[512,256]{1,0:T(8,128)(2,1)} %collective-permute-done.12.rl_ref), channel_id=1, source_target_pairs={{0,3},{1,0},{2,1},{3,2},{4,7},{5,4},{6,5},{7,6},{8,11},{9,8},{10,9... | collective-permute-start | bytes 786440 | tf_op jit(solution)/shard_map/ppermute | solution.py:267
  160.5 12.5 %collective-permute-start.15 = (bf16[512,256]{1,0:T(8,128)(2,1)}, bf16[512,256]{1,0:T(8,128)(2,1)S(1)}, u32[]{:S(2)}, u32[]{:S(2)}) collective-permute-start(bf16[512,256]{1,0:T(8,128)(2,1)} %get-tuple-element.39.up_ref), channel_id=1, source_target_pairs={{0,1},{1,2},{2,3},{3,0},{4,5},{5,6},{6,7},{7,4},{8,9},{9,10},{10,1... | collective-permute-start | bytes 786440 | tf_op jit(solution)/shard_map/ppermute | solution.py:267
  162.4 12.1 %collective-permute-start.18 = (bf16[512,256]{1,0:T(8,128)(2,1)}, bf16[512,256]{1,0:T(8,128)(2,1)S(1)}, u32[]{:S(2)}, u32[]{:S(2)}) collective-permute-start(bf16[512,256]{1,0:T(8,128)(2,1)} %get-tuple-element.40.low_ref), channel_id=1, source_target_pairs={{0,3},{1,0},{2,1},{3,2},{4,7},{5,4},{6,5},{7,6},{8,11},{9,8},{10,9... | collective-permute-start | bytes 786440 | tf_op jit(solution)/shard_map/ppermute | solution.py:267
  163.6 14.4 %all-to-all-start.3 = ((bf16[16,32,256]{2,1,0:T(8,128)(2,1)}), bf16[16,32,256]{2,1,0:T(8,128)(2,1)S(1)}, u32[]{:S(2)}, u32[]{:S(2)}) async-start(bf16[16,32,256]{2,1,0:T(8,128)(2,1)} %bitcast.12), calls=%async_computation.3 | async-start | bytes 524288 | tf_op jit(solution)/shard_map/all_to_all | solution.py:287
  171.0 11.6 %collective-permute-start.17 = (bf16[512,256]{1,0:T(8,128)(2,1)}, bf16[512,256]{1,0:T(8,128)(2,1)S(1)}, u32[]{:S(2)}, u32[]{:S(2)}) collective-permute-start(bf16[512,256]{1,0:T(8,128)(2,1)} %get-tuple-element.39.up_ref), channel_id=1, source_target_pairs={{0,3},{1,0},{2,1},{3,2},{4,7},{5,4},{6,5},{7,6},{8,11},{9,8},{10,9... | collective-permute-start | bytes 786440 | tf_op jit(solution)/shard_map/ppermute | solution.py:267
  171.2 11.4 %collective-permute-start.16 = (bf16[512,256]{1,0:T(8,128)(2,1)}, bf16[512,256]{1,0:T(8,128)(2,1)S(1)}, u32[]{:S(2)}, u32[]{:S(2)}) collective-permute-start(bf16[512,256]{1,0:T(8,128)(2,1)} %get-tuple-element.40.low_ref), channel_id=1, source_target_pairs={{0,1},{1,2},{2,3},{3,0},{4,5},{5,6},{6,7},{7,4},{8,9},{9,10},{10,1... | collective-permute-start | bytes 786440 | tf_op jit(solution)/shard_map/ppermute | solution.py:267
  173.0 14.0 %collective-permute-start.19 = (bf16[512,256]{1,0:T(8,128)(2,1)S(1)}, bf16[512,256]{1,0:T(8,128)(2,1)S(1)}, u32[]{:S(2)}, u32[]{:S(2)}) collective-permute-start(bf16[512,256]{1,0:T(8,128)(2,1)S(1)} %collective-permute-done.15.lu_ref), channel_id=1, source_target_pairs={{0,1},{1,2},{2,3},{3,0},{4,5},{5,6},{6,7},{7,4},{8,9},{9,10},{10,1... | collective-permute-start | bytes 786440 | tf_op jit(solution)/shard_map/ppermute | solution.py:267
  174.5 12.5 %collective-permute-start.20 = (bf16[512,256]{1,0:T(8,128)(2,1)S(1)}, bf16[512,256]{1,0:T(8,128)(2,1)S(1)}, u32[]{:S(2)}, u32[]{:S(2)}) collective-permute-start(bf16[512,256]{1,0:T(8,128)(2,1)S(1)} %collective-permute-done.18.rl_ref), channel_id=1, source_target_pairs={{0,3},{1,0},{2,1},{3,2},{4,7},{5,4},{6,5},{7,6},{8,11},{9,8},{10,9... | collective-permute-start | bytes 786440 | tf_op jit(solution)/shard_map/ppermute | solution.py:267
  178.7 12.4 %all-to-all-start.4 = ((f32[8,16,256]{2,1,0:T(8,128)}), f32[8,16,256]{2,1,0:T(8,128)S(1)}, u32[]{:S(2)}, u32[]{:S(2)}) async-start(f32[8,16,256]{2,1,0:T(8,128)} %convert_reduce_fusion), calls=%async_computation.4 | async-start | bytes 262144 | tf_op jit(solution)/shard_map/all_to_all | solution.py:289
  (30 other events, 148.3 us)

commit v3 on v2

--- a/solution.py
+++ b/solution.py
@@ -15,6 +15,8 @@
 BATCH = 1024
 HALF = 512
 HALO = 3072
+H = 48
+CHIPS = 8
 HIST = 2048
 ROWS = 512
 SLOTS = 12
@@ -36,7 +38,7 @@
     return math.log(strength / (layer_index + 1) + 1.0)
 
 
-def call(kernel, name, flops, mib=24, **rest):
+def call(kernel, name, flops, mib=12, **rest):
     return pl.pallas_call(
         kernel,
         name=name,
@@ -79,36 +81,47 @@
     )(ids, rows)
 
 
-def send_rest_kernel(ids_ref, zero_ref, one_ref, two_ref, send_one_ref, send_two_ref, start_ref):
-    step = pl.program_id(0)
-    chosen = one_hot_of(ids_ref[0])
-
-    @pl.when(step >= 2)
-    def _():
-        send_one_ref[...] = pick(chosen, one_ref[0])
-        send_two_ref[...] = pick(chosen, two_ref[0])
-
-    @pl.when(step < 2)
-    def _():
-        start_ref[...] = pick(chosen, zero_ref[...])
-
-
-def send_rest(ids, zero, history):
-    late = lambda i: (jnp.maximum(i - 2, 0), 0)
+def send_rest_kernel(core_ref, mine_ref, theirs_ref, own_one_ref, own_two_ref, other_ref, one_ref, two_ref):
+    for core, ids_ref, one, two in (
+        (core_ref[0], mine_ref, own_one_ref.at[0], own_two_ref.at[0]),
+        (1 - core_ref[0], theirs_ref, other_ref.at[0], other_ref.at[1]),
+    ):
+        chosen = one_hot_of(ids_ref[0])
+        one_ref[:, core] = pick(chosen, one[...]).reshape(CHIPS, H, FEAT)
+        two_ref[:, core] = pick(chosen, two[...]).reshape(CHIPS, H, FEAT)
+
+
+def send_rest(core, mine, theirs, history, other):
+    ids = pl.BlockSpec((1, BLK, CHIPS * H // BLK), lambda i: (i, 0, 0))
     whole = lambda layer: pl.BlockSpec((1, HIST, FEAT), lambda i: (layer, 0, 0))
+    rows = pl.BlockSpec((CHIPS, 2, H, FEAT), lambda i: (i, 0, 0, 0))
     return call(
         send_rest_kernel,
         "send_rest",
-        2 * (2 * HALO + BATCH) * HIST * FEAT,
-        grid=((HALO + BATCH) // ROWS,),
-        in_specs=[IDS, pl.BlockSpec((HIST, FEAT), lambda i: (0, 0)), whole(1), whole(2)],
-        out_specs=[
-            pl.BlockSpec((ROWS, FEAT), late),
-            pl.BlockSpec((ROWS, FEAT), late),
-            pl.BlockSpec((ROWS, FEAT), lambda i: (jnp.minimum(i, 1), 0)),
-        ],
-        out_shape=[shape(HALO, FEAT), shape(HALO, FEAT), shape(BATCH, FEAT)],
-    )(ids, zero, history, history)
+        4 * HALO * HIST * FEAT,
+        mib=60,
+        grid=(32 // CHIPS,),
+        in_specs=[SMEM, ids, ids, whole(1), whole(2), pl.BlockSpec((2, HIST, FEAT), lambda i: (0, 0, 0))],
+        out_specs=[rows, rows],
+        out_shape=[shape(32, 2, H, FEAT)] * 2,
+    )(core, mine, theirs, history, history, other)
+
+
+def start_kernel(ids_ref, zero_ref, out_ref):
+    out_ref[...] = pick(one_hot_of(ids_ref[0]), zero_ref[...])
+
+
+def start_rows(ids, zero):
+    return call(
+        start_kernel,
+        "start_rows",
+        flops=2 * BATCH * HIST * FEAT,
+        mib=60,
+        grid=(BATCH // ROWS,),
+        in_specs=[IDS, pl.BlockSpec((HIST, FEAT), lambda i: (0, 0))],
+        out_specs=pl.BlockSpec((ROWS, FEAT), lambda i: (i, 0)),
+        out_shape=shape(BATCH, FEAT),
+    )(ids, zero)
 
 
 def slab(w_ref, me, by):
@@ -300,17 +313,27 @@
         rows = rows.reshape(64, HALO // 64, FEAT)
         return lax.all_to_all(rows, TRAINER, 0, 0, tiled=True).reshape(HALO, FEAT)
 
+    def exchange_chips(rows):
+        rows = rows.reshape(32, 2 * H, FEAT)
+        return lax.all_to_all(rows, ("z", "x"), 0, 0, tiled=True).reshape(HALO, FEAT)
+
     zero = history[0]
     sent = send_first(send_ids, zero)
     halo = exchange(sent)
+    by_core = send_rows.reshape(32, 2, H)
+    for_core = lambda at: lax.dynamic_index_in_dim(by_core, at, 1, False)
+    by_chips = lambda ids: ids.reshape(-1, CHIPS * H // BLK, BLK).transpose(0, 2, 1)
+    other_history = shift(after(history[1:], sent), "core", 2, 1)
+    other_ids = shift(after(for_core(1 - core[0]), sent), "core", 2, 1)
     own_cot = after(cotangent, sent)
     others_cot = tuple(shift(own_cot, "y", 4, by) for by in (1, 3, 2))
-    send_one, send_two, start = send_rest(jnp.concatenate([by_step(batch_ids), send_ids], 0), zero, history)
-    halo_one = exchange(after(send_one, *others_cot))
+    send_one, send_two = send_rest(core, by_chips(for_core(core[0])), by_chips(other_ids), history, other_history)
+    start = start_rows(by_step(batch_ids), zero)
+    halo_one = exchange_chips(after(send_one, start, *others_cot))
 
     support = layer(block_cols, block_count, halves(start), halo, start, adjacency)
     one = mix(0, me, support, ring_gather(*support), weights)
-    halo_two = exchange(after(send_two, *one))
+    halo_two = exchange_chips(after(send_two, *one))
     fresh = write_rows(0, batch_ids, history, one)
     support = layer(block_cols, block_count, one, halo_one, start, adjacency)
     two = mix(1, me, support, ring_gather(*support), weights)

time: 194 us -> 189 us (0.974)
    all_to_all x3 -> x1, waiting for transfers between devices: 28.8 us -> 9.43 us  [exchange(): return lax.all_to_all(rows, TRAINER, 0, 0, tiled=True).reshape(HALO, FEAT)]
    all_to_all x0 -> x2, waiting for transfers between devices: none -> 17.2 us  [exchange_chips(): lax.all_to_all(rows, ('z', 'x'), 0, 0, tiled=True).reshape(HALO, FEAT)]
    all_to_all x3 -> x1, starting transfers between devices: 23.8 us -> 12.4 us  [exchange(): return lax.all_to_all(rows, TRAINER, 0, 0, tiled=True).reshape(HALO, FEAT)]
    all_to_all x0 -> x2, starting transfers between devices: none -> 11 us  [exchange_chips(): lax.all_to_all(rows, ('z', 'x'), 0, 0, tiled=True).reshape(HALO, FEAT)]
    unnamed x55 -> x57, local copies, waits for them, and re-layouts: 18.6 us -> 14.2 us
    ppermute x22 -> x24, waiting for transfers between devices: 31.6 us -> 34.8 us  [shift(): lax.ppermute(array, axis, [(i, (i + by) % size) for i in range(size)])]
    pallas_call x1 -> x2, Pallas kernels: 13.5 us -> 14.1 us  [the longest x1 10.6 us: send_rest(): call(send_rest_kernel, 'send_rest', 4 * HALO * HIST * FEAT, mib=60, grid=...]
    ppermute x22 -> x24, starting transfers between devices: 23 us -> 23.1 us  [shift(): lax.ppermute(array, axis, [(i, (i + by) % size) for i in range(size)])]
  transfers between devices with their start and end apart: 27 -> 29, of which waited for: 17 -> 20; matrix products, arithmetic and copies ran while one was open for 2% -> 4% of each run, Pallas kernels for 17% -> 17%
where the time goes in v3:
time: 189 us; the launch traced here: 188 us
  waiting for transfers between devices  65.1 us (34%)
  starting transfers between devices  57.5 us (30%)
  Pallas kernels  41.7 us (22%)
  local copies, waits for them, and re-layouts  21.1 us (11%)
  other arithmetic  2.09 us (1%)
    ppermute x24, waiting for transfers between devices, shift(): lax.ppermute(array, axis, [(i, (i + by) % size) for i in range(size)])  34.8 us
    ppermute x24, starting transfers between devices, shift(): lax.ppermute(array, axis, [(i, (i + by) % size) for i in range(size)])  23.1 us
    all_to_all x2, waiting for transfers between devices, exchange_chips(): lax.all_to_all(rows, ('z', 'x'), 0, 0, tiled=True).reshape(HALO, FEAT)  17.2 us
    unnamed x57, local copies, waits for them, and re-layouts  14.2 us
    all_to_all x1, starting transfers between devices, exchange(): return lax.all_to_all(rows, TRAINER, 0, 0, tiled=True).reshape(HALO, FEAT)  12.4 us
    all_to_all x2, starting transfers between devices, exchange_chips(): lax.all_to_all(rows, ('z', 'x'), 0, 0, tiled=True).reshape(HALO, FEAT)  11 us
    pallas_call x1, Pallas kernels, send_rest(): call(send_rest_kernel, 'send_rest', 4 * HALO * HIST * FEAT, mib=60, grid=...  10.6 us
    pallas_call x3, Pallas kernels, layer(): call(layer_kernel, 'layer', 2 * BATCH * SLOTS * BLK * FEAT, in_specs=[SME...  9.65 us
  transfers between devices with their start and end apart: 29, of which 20 were waited for; matrix products, arithmetic and copies ran while one was open for 4% of the time, Pallas kernels for 17%

profile of v3, /device:TPU:8, one launch (start us, length us, event | category | flops | bytes accessed | tf_op | source)
XLA Modules:
  0.0 188.4 jit_solution(7343400242995710694)
XLA Ops:
  2.3 4.6 %send_first.1 = bf16[3072,256]{1,0:T(8,128)(2,1)S(1)} custom-call(s32[6,128,4]{2,1,0:T(8,128)S(1)} %bitcast.21, bf16[2048,256]{1,0:T(8,128)(2,1)S(1)} %slice_bitcast_fusion.zero_ref.rows_ref), custom_call_target="tpu_custom_call" | custom-call | flops 3221225472 | bytes 4194304 | tf_op jit(solution)/shard_map/send_first/pallas_call | solution.py:73
  9.0 12.4 %all-to-all-start = ((bf16[64,48,256]{2,1,0:T(8,128)(2,1)}), bf16[64,48,256]{2,1,0:T(8,128)(2,1)}, u32[]{:S(2)}, u32[]{:S(2)}) async-start(bf16[64,48,256]{2,1,0:T(8,128)(2,1)} %bitcast.20), calls=%async_computation | async-start | bytes 3145728 | tf_op jit(solution)/shard_map/all_to_all | solution.py:314
  22.9 2.3 %collective-permute-start.10 = (bf16[1024,256]{1,0:T(8,128)(2,1)}, bf16[1024,256]{1,0:T(8,128)(2,1)S(1)}, u32[]{:S(2)}, u32[]{:S(2)}) collective-permute-start(bf16[1024,256]{1,0:T(8,128)(2,1)} %own_ref.1), channel_id=1, source_target_pairs={{0,2},{1,3},{2,0},{3,1},{4,6},{5,7},{6,4},{7,5},{8,10},{9,11},{10,... | collective-permute-start | bytes 1572872 | tf_op jit(solution)/shard_map/ppermute | solution.py:280
  28.2 3.5 %start_rows.1.start_ref = bf16[1024,256]{1,0:T(8,128)(2,1)} custom-call(s32[2,128,4]{2,1,0:T(8,128)} %bitcast.29, bf16[2048,256]{1,0:T(8,128)(2,1)} %copy-done.10), custom_call_target="tpu_custom_call" | custom-call | flops 1073741824 | bytes 4194304 | tf_op jit(solution)/shard_map/start_rows/pallas_call | solution.py:115
  33.6 10.6 %send_rest.1 = (bf16[32,2,48,256]{3,2,1,0:T(8,128)(2,1)}, bf16[32,2,48,256]{3,2,1,0:T(8,128)(2,1)}) custom-call(s32[1]{0:T(128)} %bitcast.7.core_ref, s32[4,128,3]{2,1,0:T(8,128)} %bitcast.27, s32[4,128,3]{2,1,0:T(8,128)} %bitcast.28, bf16[3,2048,256]{2,1,0:T(8,128)(2,1)} %history_ref.3, bf16[3,2048,256]{2,1,0:T(8,128)(2,1)} %history_ref.3, ...), custom_call_target="tpu_custom_call" | custom-call | flops 6442450944 | bytes 4194304 | tf_op jit(solution)/shard_map/send_rest/pallas_call | solution.py:98
  45.1 5.3 %collective-permute-done.8.left_ref = bf16[1024,256]{1,0:T(8,128)(2,1)S(1)} collective-permute-done((bf16[1024,256]{1,0:T(8,128)(2,1)}, bf16[1024,256]{1,0:T(8,128)(2,1)S(1)}, u32[]{:S(2)}, u32[]{:S(2)}) %collective-permute-start.8) | collective-permute-done | bytes 524320 | tf_op jit(solution)/shard_map/ppermute | solution.py:280
  52.0 9.4 %all-to-all-done = bf16[64,48,256]{2,1,0:T(8,128)(2,1)} async-done(((bf16[64,48,256]{2,1,0:T(8,128)(2,1)}), bf16[64,48,256]{2,1,0:T(8,128)(2,1)}, u32[]{:S(2)}, u32[]{:S(2)}) %all-to-all-start) | async-done | bytes 1572896 | tf_op jit(solution)/shard_map/all_to_all | solution.py:314
  61.5 5.1 %all-to-all-start.1 = ((bf16[32,96,256]{2,1,0:T(8,128)(2,1)}), bf16[32,96,256]{2,1,0:T(8,128)(2,1)}, u32[]{:S(2)}, u32[]{:S(2)}) async-start(bf16[32,96,256]{2,1,0:T(8,128)(2,1)} %bitcast.24), calls=%async_computation.1 | async-start | bytes 3145728 | tf_op jit(solution)/shard_map/all_to_all | solution.py:318
  68.7 3.4 %layer.3 = (bf16[512,256]{1,0:T(8,128)(2,1)S(1)}, bf16[512,256]{1,0:T(8,128)(2,1)}) custom-call(s32[8,12]{1,0:T(8,128)S(1)} %copy-done.25, s32[8]{0:T(128)S(1)} %copy-done.26, bf16[512,256]{1,0:T(8,128)(2,1)S(1)} %get-tuple-element.46.up_ref, bf16[512,256]{1,0:T(8,128)(2,1)S(1)} %get-tuple-element.45.low_ref, bf16[3072,256]{1,0:T(8,128)(2,1)} %bitcast.6.halo_ref, ...), custom_call_target="tpu_custom_call" | custom-call | flops 805306368 | bytes 4194304 | tf_op jit(solution)/shard_map/layer/pallas_call | solution.py:175
  76.9 4.6 %collective-permute-done.lu_ref = bf16[512,256]{1,0:T(8,128)(2,1)} collective-permute-done((bf16[512,256]{1,0:T(8,128)(2,1)S(1)}, bf16[512,256]{1,0:T(8,128)(2,1)}, u32[]{:S(2)}, u32[]{:S(2)}) %collective-permute-start) | collective-permute-done | bytes 262176 | tf_op jit(solution)/shard_map/ppermute | solution.py:280
  83.7 3.4 %collective-permute-done.1.ll_ref = bf16[512,256]{1,0:T(8,128)(2,1)} collective-permute-done((bf16[512,256]{1,0:T(8,128)(2,1)}, bf16[512,256]{1,0:T(8,128)(2,1)}, u32[]{:S(2)}, u32[]{:S(2)}) %collective-permute-start.1) | collective-permute-done | bytes 262176 | tf_op jit(solution)/shard_map/ppermute | solution.py:280
  97.8 7.7 %all-to-all-done.1 = bf16[32,96,256]{2,1,0:T(8,128)(2,1)} async-done(((bf16[32,96,256]{2,1,0:T(8,128)(2,1)}), bf16[32,96,256]{2,1,0:T(8,128)(2,1)}, u32[]{:S(2)}, u32[]{:S(2)}) %all-to-all-start.1) | async-done | bytes 1572896 | tf_op jit(solution)/shard_map/all_to_all | solution.py:318
  105.5 5.9 %all-to-all-start.2 = ((bf16[32,96,256]{2,1,0:T(8,128)(2,1)}), bf16[32,96,256]{2,1,0:T(8,128)(2,1)}, u32[]{:S(2)}, u32[]{:S(2)}) async-start(bf16[32,96,256]{2,1,0:T(8,128)(2,1)} %bitcast.23), calls=%async_computation.2 | async-start | bytes 3145728 | tf_op jit(solution)/shard_map/all_to_all | solution.py:318
  113.4 2.8 %layer.4 = (bf16[512,256]{1,0:T(8,128)(2,1)S(1)}, bf16[512,256]{1,0:T(8,128)(2,1)S(1)}) custom-call(s32[8,12]{1,0:T(8,128)S(1)} %copy-done.25, s32[8]{0:T(128)S(1)} %copy-done.26, bf16[512,256]{1,0:T(8,128)(2,1)S(1)} %get-tuple-element.26.up_ref.refs_0_, bf16[512,256]{1,0:T(8,128)(2,1)S(1)} %copy-done.12, bf16[3072,256]{1,0:T(8,128)(2,1)} %bitcast.13.halo_ref, ...), custom_call_target="tpu_custom_call" | custom-call | flops 805306368 | bytes 4194304 | tf_op jit(solution)/shard_map/layer/pallas_call | solution.py:175
  120.4 5.2 %collective-permute-done.11.lu_ref = bf16[512,256]{1,0:T(8,128)(2,1)S(1)} collective-permute-done((bf16[512,256]{1,0:T(8,128)(2,1)S(1)}, bf16[512,256]{1,0:T(8,128)(2,1)S(1)}, u32[]{:S(2)}, u32[]{:S(2)}) %collective-permute-start.11) | collective-permute-done | bytes 262176 | tf_op jit(solution)/shard_map/ppermute | solution.py:280
  127.6 2.9 %write_rows.2.refs_2_ = bf16[2,2048,256]{2,1,0:T(8,128)(2,1)} custom-call(s32[1,1024]{1,0:T(1,128)S(1)} %copy-done.24, bf16[3,2048,256]{2,1,0:T(8,128)(2,1)S(1)} %copy-done.1, bf16[512,256]{1,0:T(8,128)(2,1)S(1)} %get-tuple-element.26.up_ref.refs_0_, bf16[512,256]{1,0:T(8,128)(2,1)S(1)} %copy-done.13), custom_call_target="tpu_custom_call" | custom-call | flops 1073741824 | bytes 4194304 | tf_op jit(solution)/shard_map/write_rows/pallas_call | solution.py:240
  136.1 2.9 %write_rows.3 = bf16[2,2048,256]{2,1,0:T(8,128)(2,1)} custom-call(s32[1,1024]{1,0:T(1,128)S(1)} %copy-done.24, bf16[3,2048,256]{2,1,0:T(8,128)(2,1)S(1)} %copy-done.1, bf16[512,256]{1,0:T(8,128)(2,1)S(1)} %get-tuple-element.37.refs_0_.up_ref, bf16[512,256]{1,0:T(8,128)(2,1)S(1)} %get-tuple-element.38.refs_1_.low_ref, ...), custom_call_target="tpu_custom_call", output_to_operand_aliasing={{}: (4, {})} | custom-call | flops 1073741824 | bytes 4194304 | tf_op jit(solution)/shard_map/write_rows/pallas_call | solution.py:240
  139.8 9.5 %all-to-all-done.2 = bf16[32,96,256]{2,1,0:T(8,128)(2,1)} async-done(((bf16[32,96,256]{2,1,0:T(8,128)(2,1)}), bf16[32,96,256]{2,1,0:T(8,128)(2,1)}, u32[]{:S(2)}, u32[]{:S(2)}) %all-to-all-start.2) | async-done | bytes 1572896 | tf_op jit(solution)/shard_map/all_to_all | solution.py:318
  151.3 3.5 %layer.5 = (bf16[512,256]{1,0:T(8,128)(2,1)}, bf16[512,256]{1,0:T(8,128)(2,1)}) custom-call(s32[8,12]{1,0:T(8,128)S(1)} %copy-done.25, s32[8]{0:T(128)S(1)} %copy-done.26, bf16[512,256]{1,0:T(8,128)(2,1)S(1)} %get-tuple-element.37.refs_0_.up_ref, bf16[512,256]{1,0:T(8,128)(2,1)S(1)} %copy-done.15, bf16[3072,256]{1,0:T(8,128)(2,1)} %bitcast.15.halo_ref, ...), custom_call_target="tpu_custom_call" | custom-call | flops 805306368 | bytes 4194304 | tf_op jit(solution)/shard_map/layer/pallas_call | solution.py:175
  160.2 7.6 %all-to-all-start.3 = ((bf16[16,32,256]{2,1,0:T(8,128)(2,1)}), bf16[16,32,256]{2,1,0:T(8,128)(2,1)S(1)}, u32[]{:S(2)}, u32[]{:S(2)}) async-start(bf16[16,32,256]{2,1,0:T(8,128)(2,1)} %bitcast.16), calls=%async_computation.3 | async-start | bytes 524288 | tf_op jit(solution)/shard_map/all_to_all | solution.py:300
  171.8 2.9 %all-to-all-done.3 = bf16[16,32,256]{2,1,0:T(8,128)(2,1)S(1)} async-done(((bf16[16,32,256]{2,1,0:T(8,128)(2,1)}), bf16[16,32,256]{2,1,0:T(8,128)(2,1)S(1)}, u32[]{:S(2)}, u32[]{:S(2)}) %all-to-all-start.3) | async-done | bytes 262176 | tf_op jit(solution)/shard_map/all_to_all | solution.py:300
  175.4 3.4 %all-to-all-start.4 = ((f32[8,16,256]{2,1,0:T(8,128)}), f32[8,16,256]{2,1,0:T(8,128)S(1)}, u32[]{:S(2)}, u32[]{:S(2)}) async-start(f32[8,16,256]{2,1,0:T(8,128)} %convert_reduce_fusion), calls=%async_computation.4 | async-start | bytes 262144 | tf_op jit(solution)/shard_map/all_to_all | solution.py:302
  180.0 3.2 %collective-permute-done.21.fu_ref = bf16[512,256]{1,0:T(8,128)(2,1)S(1)} collective-permute-done((bf16[512,256]{1,0:T(8,128)(2,1)S(1)}, bf16[512,256]{1,0:T(8,128)(2,1)S(1)}, u32[]{:S(2)}, u32[]{:S(2)}) %collective-permute-start.21) | collective-permute-done | bytes 262176 | tf_op jit(solution)/shard_map/ppermute | solution.py:280
  184.6 2.5 %mix_last.1 = bf16[1024,256]{1,0:T(8,128)(2,1)} custom-call(s32[1]{0:T(128)} %bitcast.me_ref, bf16[512,256]{1,0:T(8,128)(2,1)} %get-tuple-element.41.up_ref, bf16[512,256]{1,0:T(8,128)(2,1)} %get-tuple-element.42.low_ref, bf16[512,256]{1,0:T(8,128)(2,1)S(1)} %collective-permute-done.17.lu_ref, bf16[512,256]{1,0:T(8,128)(2,1)S(1)} %collective-permute-done.18.ll_ref, ...), custom_call_target="tpu_custom_call" | custom-call | flops 99999997952 | bytes 4194304 | tf_op jit(solution)/shard_map/mix_last/pallas_call | solution.py:213
  (118 shorter events, 62.9 us)
Async XLA Ops:
  9.0 52.4 %all-to-all-start = ((bf16[64,48,256]{2,1,0:T(8,128)(2,1)}), bf16[64,48,256]{2,1,0:T(8,128)(2,1)}, u32[]{:S(2)}, u32[]{:S(2)}) async-start(bf16[64,48,256]{2,1,0:T(8,128)(2,1)} %bitcast.20), calls=%async_computation | async-start | bytes 3145728 | tf_op jit(solution)/shard_map/all_to_all | solution.py:314
  22.9 10.7 %collective-permute-start.7 = (bf16[2,2048,256]{2,1,0:T(8,128)(2,1)}, bf16[2,2048,256]{2,1,0:T(8,128)(2,1)}, u32[]{:S(2)}, u32[]{:S(2)}) collective-permute-start(bf16[2,2048,256]{2,1,0:T(8,128)(2,1)} %slice.15), channel_id=1, source_target_pairs={{0,4},{4,0},{1,5},{5,1},{2,6},{6,2},{3,7},{7,3},{8,12},{12,8},{9,1... | collective-permute-start | bytes 6291464 | tf_op jit(solution)/shard_map/ppermute | solution.py:280
  22.9 21.3 %collective-permute-start.10 = (bf16[1024,256]{1,0:T(8,128)(2,1)}, bf16[1024,256]{1,0:T(8,128)(2,1)S(1)}, u32[]{:S(2)}, u32[]{:S(2)}) collective-permute-start(bf16[1024,256]{1,0:T(8,128)(2,1)} %own_ref.1), channel_id=1, source_target_pairs={{0,2},{1,3},{2,0},{3,1},{4,6},{5,7},{6,4},{7,5},{8,10},{9,11},{10,... | collective-permute-start | bytes 1572872 | tf_op jit(solution)/shard_map/ppermute | solution.py:280
  25.2 25.1 %collective-permute-start.8 = (bf16[1024,256]{1,0:T(8,128)(2,1)}, bf16[1024,256]{1,0:T(8,128)(2,1)S(1)}, u32[]{:S(2)}, u32[]{:S(2)}) collective-permute-start(bf16[1024,256]{1,0:T(8,128)(2,1)} %own_ref.1), channel_id=1, source_target_pairs={{0,1},{1,2},{2,3},{3,0},{4,5},{5,6},{6,7},{7,4},{8,9},{9,10},{10,1... | collective-permute-start | bytes 1572872 | tf_op jit(solution)/shard_map/ppermute | solution.py:280
  25.2 26.0 %collective-permute-start.9 = (bf16[1024,256]{1,0:T(8,128)(2,1)}, bf16[1024,256]{1,0:T(8,128)(2,1)S(1)}, u32[]{:S(2)}, u32[]{:S(2)}) collective-permute-start(bf16[1024,256]{1,0:T(8,128)(2,1)} %own_ref.1), channel_id=1, source_target_pairs={{0,3},{1,0},{2,1},{3,2},{4,7},{5,4},{6,5},{7,6},{8,11},{9,8},{10,9... | collective-permute-start | bytes 1572872 | tf_op jit(solution)/shard_map/ppermute | solution.py:280
  61.5 44.1 %all-to-all-start.1 = ((bf16[32,96,256]{2,1,0:T(8,128)(2,1)}), bf16[32,96,256]{2,1,0:T(8,128)(2,1)}, u32[]{:S(2)}, u32[]{:S(2)}) async-start(bf16[32,96,256]{2,1,0:T(8,128)(2,1)} %bitcast.24), calls=%async_computation.1 | async-start | bytes 3145728 | tf_op jit(solution)/shard_map/all_to_all | solution.py:318
  72.1 9.3 %collective-permute-start = (bf16[512,256]{1,0:T(8,128)(2,1)S(1)}, bf16[512,256]{1,0:T(8,128)(2,1)}, u32[]{:S(2)}, u32[]{:S(2)}) collective-permute-start(bf16[512,256]{1,0:T(8,128)(2,1)S(1)} %get-tuple-element.24.up_ref), channel_id=1, source_target_pairs={{0,1},{1,2},{2,3},{3,0},{4,5},{5,6},{6,7},{7,4},{8,9},{9,10},{10,1... | collective-permute-start | bytes 786440 | tf_op jit(solution)/shard_map/ppermute | solution.py:280
  73.7 9.6 %collective-permute-start.3 = (bf16[512,256]{1,0:T(8,128)(2,1)}, bf16[512,256]{1,0:T(8,128)(2,1)}, u32[]{:S(2)}, u32[]{:S(2)}) collective-permute-start(bf16[512,256]{1,0:T(8,128)(2,1)} %get-tuple-element.25.low_ref), channel_id=1, source_target_pairs={{0,3},{1,0},{2,1},{3,2},{4,7},{5,4},{6,5},{7,6},{8,11},{9,8},{10,9... | collective-permute-start | bytes 786440 | tf_op jit(solution)/shard_map/ppermute | solution.py:280
  74.1 12.9 %collective-permute-start.1 = (bf16[512,256]{1,0:T(8,128)(2,1)}, bf16[512,256]{1,0:T(8,128)(2,1)}, u32[]{:S(2)}, u32[]{:S(2)}) collective-permute-start(bf16[512,256]{1,0:T(8,128)(2,1)} %get-tuple-element.25.low_ref), channel_id=1, source_target_pairs={{0,1},{1,2},{2,3},{3,0},{4,5},{5,6},{6,7},{7,4},{8,9},{9,10},{10,1... | collective-permute-start | bytes 786440 | tf_op jit(solution)/shard_map/ppermute | solution.py:280
  75.7 13.2 %collective-permute-start.2 = (bf16[512,256]{1,0:T(8,128)(2,1)S(1)}, bf16[512,256]{1,0:T(8,128)(2,1)}, u32[]{:S(2)}, u32[]{:S(2)}) collective-permute-start(bf16[512,256]{1,0:T(8,128)(2,1)S(1)} %get-tuple-element.24.up_ref), channel_id=1, source_target_pairs={{0,3},{1,0},{2,1},{3,2},{4,7},{5,4},{6,5},{7,6},{8,11},{9,8},{10,9... | collective-permute-start | bytes 786440 | tf_op jit(solution)/shard_map/ppermute | solution.py:280
  81.4 9.6 %collective-permute-start.4 = (bf16[512,256]{1,0:T(8,128)(2,1)}, bf16[512,256]{1,0:T(8,128)(2,1)}, u32[]{:S(2)}, u32[]{:S(2)}) collective-permute-start(bf16[512,256]{1,0:T(8,128)(2,1)} %collective-permute-done.lu_ref), channel_id=1, source_target_pairs={{0,1},{1,2},{2,3},{3,0},{4,5},{5,6},{6,7},{7,4},{8,9},{9,10},{10,1... | collective-permute-start | bytes 786440 | tf_op jit(solution)/shard_map/ppermute | solution.py:280
  83.2 9.4 %collective-permute-start.5 = (bf16[512,256]{1,0:T(8,128)(2,1)}, bf16[512,256]{1,0:T(8,128)(2,1)}, u32[]{:S(2)}, u32[]{:S(2)}) collective-permute-start(bf16[512,256]{1,0:T(8,128)(2,1)} %collective-permute-done.3.rl_ref), channel_id=1, source_target_pairs={{0,3},{1,0},{2,1},{3,2},{4,7},{5,4},{6,5},{7,6},{8,11},{9,8},{10,9... | collective-permute-start | bytes 786440 | tf_op jit(solution)/shard_map/ppermute | solution.py:280
  105.5 43.8 %all-to-all-start.2 = ((bf16[32,96,256]{2,1,0:T(8,128)(2,1)}), bf16[32,96,256]{2,1,0:T(8,128)(2,1)}, u32[]{:S(2)}, u32[]{:S(2)}) async-start(bf16[32,96,256]{2,1,0:T(8,128)(2,1)} %bitcast.23), calls=%async_computation.2 | async-start | bytes 3145728 | tf_op jit(solution)/shard_map/all_to_all | solution.py:318
  116.2 9.3 %collective-permute-start.11 = (bf16[512,256]{1,0:T(8,128)(2,1)S(1)}, bf16[512,256]{1,0:T(8,128)(2,1)S(1)}, u32[]{:S(2)}, u32[]{:S(2)}) collective-permute-start(bf16[512,256]{1,0:T(8,128)(2,1)S(1)} %get-tuple-element.33.up_ref), channel_id=1, source_target_pairs={{0,1},{1,2},{2,3},{3,0},{4,5},{5,6},{6,7},{7,4},{8,9},{9,10},{10,1... | collective-permute-start | bytes 786440 | tf_op jit(solution)/shard_map/ppermute | solution.py:280
  118.3 12.8 %collective-permute-start.12 = (bf16[512,256]{1,0:T(8,128)(2,1)S(1)}, bf16[512,256]{1,0:T(8,128)(2,1)S(1)}, u32[]{:S(2)}, u32[]{:S(2)}) collective-permute-start(bf16[512,256]{1,0:T(8,128)(2,1)S(1)} %get-tuple-element.34.low_ref), channel_id=1, source_target_pairs={{0,1},{1,2},{2,3},{3,0},{4,5},{5,6},{6,7},{7,4},{8,9},{9,10},{10,1... | collective-permute-start | bytes 786440 | tf_op jit(solution)/shard_map/ppermute | solution.py:280
  119.9 12.7 %collective-permute-start.13 = (bf16[512,256]{1,0:T(8,128)(2,1)S(1)}, bf16[512,256]{1,0:T(8,128)(2,1)S(1)}, u32[]{:S(2)}, u32[]{:S(2)}) collective-permute-start(bf16[512,256]{1,0:T(8,128)(2,1)S(1)} %get-tuple-element.33.up_ref), channel_id=1, source_target_pairs={{0,3},{1,0},{2,1},{3,2},{4,7},{5,4},{6,5},{7,6},{8,11},{9,8},{10,9... | collective-permute-start | bytes 786440 | tf_op jit(solution)/shard_map/ppermute | solution.py:280
  157.1 12.7 %collective-permute-start.17 = (bf16[512,256]{1,0:T(8,128)(2,1)}, bf16[512,256]{1,0:T(8,128)(2,1)S(1)}, u32[]{:S(2)}, u32[]{:S(2)}) collective-permute-start(bf16[512,256]{1,0:T(8,128)(2,1)} %get-tuple-element.41.up_ref), channel_id=1, source_target_pairs={{0,1},{1,2},{2,3},{3,0},{4,5},{5,6},{6,7},{7,4},{8,9},{9,10},{10,1... | collective-permute-start | bytes 786440 | tf_op jit(solution)/shard_map/ppermute | solution.py:280
  158.9 12.3 %collective-permute-start.20 = (bf16[512,256]{1,0:T(8,128)(2,1)}, bf16[512,256]{1,0:T(8,128)(2,1)S(1)}, u32[]{:S(2)}, u32[]{:S(2)}) collective-permute-start(bf16[512,256]{1,0:T(8,128)(2,1)} %get-tuple-element.42.low_ref), channel_id=1, source_target_pairs={{0,3},{1,0},{2,1},{3,2},{4,7},{5,4},{6,5},{7,6},{8,11},{9,8},{10,9... | collective-permute-start | bytes 786440 | tf_op jit(solution)/shard_map/ppermute | solution.py:280
  160.2 14.6 %all-to-all-start.3 = ((bf16[16,32,256]{2,1,0:T(8,128)(2,1)}), bf16[16,32,256]{2,1,0:T(8,128)(2,1)S(1)}, u32[]{:S(2)}, u32[]{:S(2)}) async-start(bf16[16,32,256]{2,1,0:T(8,128)(2,1)} %bitcast.16), calls=%async_computation.3 | async-start | bytes 524288 | tf_op jit(solution)/shard_map/all_to_all | solution.py:300
  167.7 11.1 %collective-permute-start.18 = (bf16[512,256]{1,0:T(8,128)(2,1)}, bf16[512,256]{1,0:T(8,128)(2,1)S(1)}, u32[]{:S(2)}, u32[]{:S(2)}) collective-permute-start(bf16[512,256]{1,0:T(8,128)(2,1)} %get-tuple-element.42.low_ref), channel_id=1, source_target_pairs={{0,1},{1,2},{2,3},{3,0},{4,5},{5,6},{6,7},{7,4},{8,9},{9,10},{10,1... | collective-permute-start | bytes 786440 | tf_op jit(solution)/shard_map/ppermute | solution.py:280
  169.2 10.8 %collective-permute-start.19 = (bf16[512,256]{1,0:T(8,128)(2,1)}, bf16[512,256]{1,0:T(8,128)(2,1)S(1)}, u32[]{:S(2)}, u32[]{:S(2)}) collective-permute-start(bf16[512,256]{1,0:T(8,128)(2,1)} %get-tuple-element.41.up_ref), channel_id=1, source_target_pairs={{0,3},{1,0},{2,1},{3,2},{4,7},{5,4},{6,5},{7,6},{8,11},{9,8},{10,9... | collective-permute-start | bytes 786440 | tf_op jit(solution)/shard_map/ppermute | solution.py:280
  169.8 13.4 %collective-permute-start.21 = (bf16[512,256]{1,0:T(8,128)(2,1)S(1)}, bf16[512,256]{1,0:T(8,128)(2,1)S(1)}, u32[]{:S(2)}, u32[]{:S(2)}) collective-permute-start(bf16[512,256]{1,0:T(8,128)(2,1)S(1)} %collective-permute-done.17.lu_ref), channel_id=1, source_target_pairs={{0,1},{1,2},{2,3},{3,0},{4,5},{5,6},{6,7},{7,4},{8,9},{9,10},{10,1... | collective-permute-start | bytes 786440 | tf_op jit(solution)/shard_map/ppermute | solution.py:280
  171.2 13.3 %collective-permute-start.22 = (bf16[512,256]{1,0:T(8,128)(2,1)S(1)}, bf16[512,256]{1,0:T(8,128)(2,1)S(1)}, u32[]{:S(2)}, u32[]{:S(2)}) collective-permute-start(bf16[512,256]{1,0:T(8,128)(2,1)S(1)} %collective-permute-done.20.rl_ref), channel_id=1, source_target_pairs={{0,3},{1,0},{2,1},{3,2},{4,7},{5,4},{6,5},{7,6},{8,11},{9,8},{10,9... | collective-permute-start | bytes 786440 | tf_op jit(solution)/shard_map/ppermute | solution.py:280
  175.4 12.4 %all-to-all-start.4 = ((f32[8,16,256]{2,1,0:T(8,128)}), f32[8,16,256]{2,1,0:T(8,128)S(1)}, u32[]{:S(2)}, u32[]{:S(2)}) async-start(f32[8,16,256]{2,1,0:T(8,128)} %convert_reduce_fusion), calls=%async_computation.4 | async-start | bytes 262144 | tf_op jit(solution)/shard_map/all_to_all | solution.py:302
  (33 other events, 172.3 us)

commit v4 on v3

--- a/solution.py
+++ b/solution.py
@@ -19,6 +19,7 @@
 CHIPS = 8
 HIST = 2048
 ROWS = 512
+TALL = 1024
 SLOTS = 12
 RB = 8
 HB = HALO // BLK
@@ -74,9 +75,10 @@
         send_first_kernel,
         "send_first",
         2 * HALO * HIST * FEAT,
-        grid=(HALO // ROWS,),
-        in_specs=[IDS, pl.BlockSpec((HIST, FEAT), lambda i: (0, 0))],
-        out_specs=pl.BlockSpec((ROWS, FEAT), lambda i: (i, 0)),
+        mib=24,
+        grid=(HALO // TALL,),
+        in_specs=[pl.BlockSpec((1, BLK, TALL // BLK), lambda i: (i, 0, 0)), pl.BlockSpec((HIST, FEAT), lambda i: (0, 0))],
+        out_specs=pl.BlockSpec((TALL, FEAT), lambda i: (i, 0)),
         out_shape=shape(HALO, FEAT),
     )(ids, rows)
 
@@ -307,7 +309,7 @@
     me = lax.axis_index("y").astype(jnp.int32).reshape(1)
     core = lax.axis_index("core").astype(jnp.int32).reshape(1)
     by_step = lambda ids: ids.reshape(-1, ROWS // BLK, BLK).transpose(0, 2, 1)
-    send_ids = by_step(send_rows)
+    send_ids = send_rows.reshape(-1, TALL // BLK, BLK).transpose(0, 2, 1)
 
     def exchange(rows):
         rows = rows.reshape(64, HALO // 64, FEAT)

time: 189 us -> 189 us (level)
  no operation moved by 1% of the time
where the time goes in v4:
time: 189 us; the launch traced here: 188 us
  waiting for transfers between devices  65.3 us (35%)
  starting transfers between devices  57.5 us (30%)
  Pallas kernels  41.1 us (22%)
  local copies, waits for them, and re-layouts  21 us (11%)
  other arithmetic  2.09 us (1%)
    ppermute x24, waiting for transfers between devices, shift(): lax.ppermute(array, axis, [(i, (i + by) % size) for i in range(size)])  34.7 us
    ppermute x24, starting transfers between devices, shift(): lax.ppermute(array, axis, [(i, (i + by) % size) for i in range(size)])  23.1 us
    all_to_all x2, waiting for transfers between devices, exchange_chips(): lax.all_to_all(rows, ('z', 'x'), 0, 0, tiled=True).reshape(HALO, FEAT)  17.2 us
    unnamed x57, local copies, waits for them, and re-layouts  14.2 us
    all_to_all x1, starting transfers between devices, exchange(): return lax.all_to_all(rows, TRAINER, 0, 0, tiled=True).reshape(HALO, FEAT)  12.4 us
    all_to_all x2, starting transfers between devices, exchange_chips(): lax.all_to_all(rows, ('z', 'x'), 0, 0, tiled=True).reshape(HALO, FEAT)  11 us
    pallas_call x1, Pallas kernels, send_rest(): call(send_rest_kernel, 'send_rest', 4 * HALO * HIST * FEAT, mib=60, grid=...  10.6 us
    pallas_call x3, Pallas kernels, layer(): call(layer_kernel, 'layer', 2 * BATCH * SLOTS * BLK * FEAT, in_specs=[SME...  9.65 us
  transfers between devices with their start and end apart: 29, of which 20 were waited for; matrix products, arithmetic and copies ran while one was open for 4% of the time, Pallas kernels for 17%

profile of v4, /device:TPU:8, one launch (start us, length us, event | category | flops | bytes accessed | tf_op | source)
XLA Modules:
  0.0 187.9 jit_solution(11706528079657463244)
XLA Ops:
  2.2 3.9 %send_first.1 = bf16[3072,256]{1,0:T(8,128)(2,1)S(1)} custom-call(s32[3,128,8]{2,1,0:T(8,128)S(1)} %bitcast.21, bf16[2048,256]{1,0:T(8,128)(2,1)S(1)} %slice_bitcast_fusion.zero_ref.rows_ref), custom_call_target="tpu_custom_call" | custom-call | flops 3221225472 | bytes 4194304 | tf_op jit(solution)/shard_map/send_first/pallas_call | solution.py:74
  8.3 12.4 %all-to-all-start = ((bf16[64,48,256]{2,1,0:T(8,128)(2,1)}), bf16[64,48,256]{2,1,0:T(8,128)(2,1)}, u32[]{:S(2)}, u32[]{:S(2)}) async-start(bf16[64,48,256]{2,1,0:T(8,128)(2,1)} %bitcast.20), calls=%async_computation | async-start | bytes 3145728 | tf_op jit(solution)/shard_map/all_to_all | solution.py:316
  22.2 2.3 %collective-permute-start.10 = (bf16[1024,256]{1,0:T(8,128)(2,1)}, bf16[1024,256]{1,0:T(8,128)(2,1)S(1)}, u32[]{:S(2)}, u32[]{:S(2)}) collective-permute-start(bf16[1024,256]{1,0:T(8,128)(2,1)} %own_ref.1), channel_id=1, source_target_pairs={{0,2},{1,3},{2,0},{3,1},{4,6},{5,7},{6,4},{7,5},{8,10},{9,11},{10,... | collective-permute-start | bytes 1572872 | tf_op jit(solution)/shard_map/ppermute | solution.py:282
  27.5 3.5 %start_rows.1.start_ref = bf16[1024,256]{1,0:T(8,128)(2,1)} custom-call(s32[2,128,4]{2,1,0:T(8,128)} %bitcast.29, bf16[2048,256]{1,0:T(8,128)(2,1)} %copy-done.10), custom_call_target="tpu_custom_call" | custom-call | flops 1073741824 | bytes 4194304 | tf_op jit(solution)/shard_map/start_rows/pallas_call | solution.py:117
  32.9 10.6 %send_rest.1 = (bf16[32,2,48,256]{3,2,1,0:T(8,128)(2,1)}, bf16[32,2,48,256]{3,2,1,0:T(8,128)(2,1)}) custom-call(s32[1]{0:T(128)} %bitcast.7.core_ref, s32[4,128,3]{2,1,0:T(8,128)} %bitcast.27, s32[4,128,3]{2,1,0:T(8,128)} %bitcast.28, bf16[3,2048,256]{2,1,0:T(8,128)(2,1)} %history_ref.3, bf16[3,2048,256]{2,1,0:T(8,128)(2,1)} %history_ref.3, ...), custom_call_target="tpu_custom_call" | custom-call | flops 6442450944 | bytes 4194304 | tf_op jit(solution)/shard_map/send_rest/pallas_call | solution.py:100
  44.3 5.3 %collective-permute-done.8.left_ref = bf16[1024,256]{1,0:T(8,128)(2,1)S(1)} collective-permute-done((bf16[1024,256]{1,0:T(8,128)(2,1)}, bf16[1024,256]{1,0:T(8,128)(2,1)S(1)}, u32[]{:S(2)}, u32[]{:S(2)}) %collective-permute-start.8) | collective-permute-done | bytes 524320 | tf_op jit(solution)/shard_map/ppermute | solution.py:282
  51.3 9.4 %all-to-all-done = bf16[64,48,256]{2,1,0:T(8,128)(2,1)} async-done(((bf16[64,48,256]{2,1,0:T(8,128)(2,1)}), bf16[64,48,256]{2,1,0:T(8,128)(2,1)}, u32[]{:S(2)}, u32[]{:S(2)}) %all-to-all-start) | async-done | bytes 1572896 | tf_op jit(solution)/shard_map/all_to_all | solution.py:316
  60.7 5.1 %all-to-all-start.1 = ((bf16[32,96,256]{2,1,0:T(8,128)(2,1)}), bf16[32,96,256]{2,1,0:T(8,128)(2,1)}, u32[]{:S(2)}, u32[]{:S(2)}) async-start(bf16[32,96,256]{2,1,0:T(8,128)(2,1)} %bitcast.24), calls=%async_computation.1 | async-start | bytes 3145728 | tf_op jit(solution)/shard_map/all_to_all | solution.py:320
  68.0 3.4 %layer.3 = (bf16[512,256]{1,0:T(8,128)(2,1)S(1)}, bf16[512,256]{1,0:T(8,128)(2,1)}) custom-call(s32[8,12]{1,0:T(8,128)S(1)} %copy-done.25, s32[8]{0:T(128)S(1)} %copy-done.26, bf16[512,256]{1,0:T(8,128)(2,1)S(1)} %get-tuple-element.46.up_ref, bf16[512,256]{1,0:T(8,128)(2,1)S(1)} %get-tuple-element.45.low_ref, bf16[3072,256]{1,0:T(8,128)(2,1)} %bitcast.6.halo_ref, ...), custom_call_target="tpu_custom_call" | custom-call | flops 805306368 | bytes 4194304 | tf_op jit(solution)/shard_map/layer/pallas_call | solution.py:177
  76.1 4.6 %collective-permute-done.lu_ref = bf16[512,256]{1,0:T(8,128)(2,1)} collective-permute-done((bf16[512,256]{1,0:T(8,128)(2,1)S(1)}, bf16[512,256]{1,0:T(8,128)(2,1)}, u32[]{:S(2)}, u32[]{:S(2)}) %collective-permute-start) | collective-permute-done | bytes 262176 | tf_op jit(solution)/shard_map/ppermute | solution.py:282
  82.9 3.4 %collective-permute-done.1.ll_ref = bf16[512,256]{1,0:T(8,128)(2,1)} collective-permute-done((bf16[512,256]{1,0:T(8,128)(2,1)}, bf16[512,256]{1,0:T(8,128)(2,1)}, u32[]{:S(2)}, u32[]{:S(2)}) %collective-permute-start.1) | collective-permute-done | bytes 262176 | tf_op jit(solution)/shard_map/ppermute | solution.py:282
  97.1 7.7 %all-to-all-done.1 = bf16[32,96,256]{2,1,0:T(8,128)(2,1)} async-done(((bf16[32,96,256]{2,1,0:T(8,128)(2,1)}), bf16[32,96,256]{2,1,0:T(8,128)(2,1)}, u32[]{:S(2)}, u32[]{:S(2)}) %all-to-all-start.1) | async-done | bytes 1572896 | tf_op jit(solution)/shard_map/all_to_all | solution.py:320
  104.8 5.9 %all-to-all-start.2 = ((bf16[32,96,256]{2,1,0:T(8,128)(2,1)}), bf16[32,96,256]{2,1,0:T(8,128)(2,1)}, u32[]{:S(2)}, u32[]{:S(2)}) async-start(bf16[32,96,256]{2,1,0:T(8,128)(2,1)} %bitcast.23), calls=%async_computation.2 | async-start | bytes 3145728 | tf_op jit(solution)/shard_map/all_to_all | solution.py:320
  112.7 2.8 %layer.4 = (bf16[512,256]{1,0:T(8,128)(2,1)S(1)}, bf16[512,256]{1,0:T(8,128)(2,1)S(1)}) custom-call(s32[8,12]{1,0:T(8,128)S(1)} %copy-done.25, s32[8]{0:T(128)S(1)} %copy-done.26, bf16[512,256]{1,0:T(8,128)(2,1)S(1)} %get-tuple-element.26.up_ref.refs_0_, bf16[512,256]{1,0:T(8,128)(2,1)S(1)} %copy-done.12, bf16[3072,256]{1,0:T(8,128)(2,1)} %bitcast.13.halo_ref, ...), custom_call_target="tpu_custom_call" | custom-call | flops 805306368 | bytes 4194304 | tf_op jit(solution)/shard_map/layer/pallas_call | solution.py:177
  119.6 5.2 %collective-permute-done.11.lu_ref = bf16[512,256]{1,0:T(8,128)(2,1)S(1)} collective-permute-done((bf16[512,256]{1,0:T(8,128)(2,1)S(1)}, bf16[512,256]{1,0:T(8,128)(2,1)S(1)}, u32[]{:S(2)}, u32[]{:S(2)}) %collective-permute-start.11) | collective-permute-done | bytes 262176 | tf_op jit(solution)/shard_map/ppermute | solution.py:282
  126.9 2.9 %write_rows.2.refs_2_ = bf16[2,2048,256]{2,1,0:T(8,128)(2,1)} custom-call(s32[1,1024]{1,0:T(1,128)S(1)} %copy-done.24, bf16[3,2048,256]{2,1,0:T(8,128)(2,1)S(1)} %copy-done.1, bf16[512,256]{1,0:T(8,128)(2,1)S(1)} %get-tuple-element.26.up_ref.refs_0_, bf16[512,256]{1,0:T(8,128)(2,1)S(1)} %copy-done.13), custom_call_target="tpu_custom_call" | custom-call | flops 1073741824 | bytes 4194304 | tf_op jit(solution)/shard_map/write_rows/pallas_call | solution.py:242
  135.4 2.9 %write_rows.3 = bf16[2,2048,256]{2,1,0:T(8,128)(2,1)} custom-call(s32[1,1024]{1,0:T(1,128)S(1)} %copy-done.24, bf16[3,2048,256]{2,1,0:T(8,128)(2,1)S(1)} %copy-done.1, bf16[512,256]{1,0:T(8,128)(2,1)S(1)} %get-tuple-element.37.refs_0_.up_ref, bf16[512,256]{1,0:T(8,128)(2,1)S(1)} %get-tuple-element.38.refs_1_.low_ref, ...), custom_call_target="tpu_custom_call", output_to_operand_aliasing={{}: (4, {})} | custom-call | flops 1073741824 | bytes 4194304 | tf_op jit(solution)/shard_map/write_rows/pallas_call | solution.py:242
  139.1 9.5 %all-to-all-done.2 = bf16[32,96,256]{2,1,0:T(8,128)(2,1)} async-done(((bf16[32,96,256]{2,1,0:T(8,128)(2,1)}), bf16[32,96,256]{2,1,0:T(8,128)(2,1)}, u32[]{:S(2)}, u32[]{:S(2)}) %all-to-all-start.2) | async-done | bytes 1572896 | tf_op jit(solution)/shard_map/all_to_all | solution.py:320
  150.6 3.5 %layer.5 = (bf16[512,256]{1,0:T(8,128)(2,1)}, bf16[512,256]{1,0:T(8,128)(2,1)}) custom-call(s32[8,12]{1,0:T(8,128)S(1)} %copy-done.25, s32[8]{0:T(128)S(1)} %copy-done.26, bf16[512,256]{1,0:T(8,128)(2,1)S(1)} %get-tuple-element.37.refs_0_.up_ref, bf16[512,256]{1,0:T(8,128)(2,1)S(1)} %copy-done.15, bf16[3072,256]{1,0:T(8,128)(2,1)} %bitcast.15.halo_ref, ...), custom_call_target="tpu_custom_call" | custom-call | flops 805306368 | bytes 4194304 | tf_op jit(solution)/shard_map/layer/pallas_call | solution.py:177
  159.4 7.6 %all-to-all-start.3 = ((bf16[16,32,256]{2,1,0:T(8,128)(2,1)}), bf16[16,32,256]{2,1,0:T(8,128)(2,1)S(1)}, u32[]{:S(2)}, u32[]{:S(2)}) async-start(bf16[16,32,256]{2,1,0:T(8,128)(2,1)} %bitcast.16), calls=%async_computation.3 | async-start | bytes 524288 | tf_op jit(solution)/shard_map/all_to_all | solution.py:302
  171.1 3.2 %all-to-all-done.3 = bf16[16,32,256]{2,1,0:T(8,128)(2,1)S(1)} async-done(((bf16[16,32,256]{2,1,0:T(8,128)(2,1)}), bf16[16,32,256]{2,1,0:T(8,128)(2,1)S(1)}, u32[]{:S(2)}, u32[]{:S(2)}) %all-to-all-start.3) | async-done | bytes 262176 | tf_op jit(solution)/shard_map/all_to_all | solution.py:302
  174.9 3.4 %all-to-all-start.4 = ((f32[8,16,256]{2,1,0:T(8,128)}), f32[8,16,256]{2,1,0:T(8,128)S(1)}, u32[]{:S(2)}, u32[]{:S(2)}) async-start(f32[8,16,256]{2,1,0:T(8,128)} %convert_reduce_fusion), calls=%async_computation.4 | async-start | bytes 262144 | tf_op jit(solution)/shard_map/all_to_all | solution.py:304
  179.4 3.1 %collective-permute-done.21.fu_ref = bf16[512,256]{1,0:T(8,128)(2,1)S(1)} collective-permute-done((bf16[512,256]{1,0:T(8,128)(2,1)S(1)}, bf16[512,256]{1,0:T(8,128)(2,1)S(1)}, u32[]{:S(2)}, u32[]{:S(2)}) %collective-permute-start.21) | collective-permute-done | bytes 262176 | tf_op jit(solution)/shard_map/ppermute | solution.py:282
  183.9 2.5 %mix_last.1 = bf16[1024,256]{1,0:T(8,128)(2,1)} custom-call(s32[1]{0:T(128)} %bitcast.me_ref, bf16[512,256]{1,0:T(8,128)(2,1)} %get-tuple-element.41.up_ref, bf16[512,256]{1,0:T(8,128)(2,1)} %get-tuple-element.42.low_ref, bf16[512,256]{1,0:T(8,128)(2,1)S(1)} %collective-permute-done.17.lu_ref, bf16[512,256]{1,0:T(8,128)(2,1)S(1)} %collective-permute-done.18.ll_ref, ...), custom_call_target="tpu_custom_call" | custom-call | flops 99999997952 | bytes 4194304 | tf_op jit(solution)/shard_map/mix_last/pallas_call | solution.py:215
  (118 shorter events, 63.0 us)
Async XLA Ops:
  8.3 52.4 %all-to-all-start = ((bf16[64,48,256]{2,1,0:T(8,128)(2,1)}), bf16[64,48,256]{2,1,0:T(8,128)(2,1)}, u32[]{:S(2)}, u32[]{:S(2)}) async-start(bf16[64,48,256]{2,1,0:T(8,128)(2,1)} %bitcast.20), calls=%async_computation | async-start | bytes 3145728 | tf_op jit(solution)/shard_map/all_to_all | solution.py:316
  22.2 10.7 %collective-permute-start.7 = (bf16[2,2048,256]{2,1,0:T(8,128)(2,1)}, bf16[2,2048,256]{2,1,0:T(8,128)(2,1)}, u32[]{:S(2)}, u32[]{:S(2)}) collective-permute-start(bf16[2,2048,256]{2,1,0:T(8,128)(2,1)} %slice.15), channel_id=1, source_target_pairs={{0,4},{4,0},{1,5},{5,1},{2,6},{6,2},{3,7},{7,3},{8,12},{12,8},{9,1... | collective-permute-start | bytes 6291464 | tf_op jit(solution)/shard_map/ppermute | solution.py:282
  22.2 21.3 %collective-permute-start.10 = (bf16[1024,256]{1,0:T(8,128)(2,1)}, bf16[1024,256]{1,0:T(8,128)(2,1)S(1)}, u32[]{:S(2)}, u32[]{:S(2)}) collective-permute-start(bf16[1024,256]{1,0:T(8,128)(2,1)} %own_ref.1), channel_id=1, source_target_pairs={{0,2},{1,3},{2,0},{3,1},{4,6},{5,7},{6,4},{7,5},{8,10},{9,11},{10,... | collective-permute-start | bytes 1572872 | tf_op jit(solution)/shard_map/ppermute | solution.py:282
  24.5 25.1 %collective-permute-start.8 = (bf16[1024,256]{1,0:T(8,128)(2,1)}, bf16[1024,256]{1,0:T(8,128)(2,1)S(1)}, u32[]{:S(2)}, u32[]{:S(2)}) collective-permute-start(bf16[1024,256]{1,0:T(8,128)(2,1)} %own_ref.1), channel_id=1, source_target_pairs={{0,1},{1,2},{2,3},{3,0},{4,5},{5,6},{6,7},{7,4},{8,9},{9,10},{10,1... | collective-permute-start | bytes 1572872 | tf_op jit(solution)/shard_map/ppermute | solution.py:282
  24.5 26.0 %collective-permute-start.9 = (bf16[1024,256]{1,0:T(8,128)(2,1)}, bf16[1024,256]{1,0:T(8,128)(2,1)S(1)}, u32[]{:S(2)}, u32[]{:S(2)}) collective-permute-start(bf16[1024,256]{1,0:T(8,128)(2,1)} %own_ref.1), channel_id=1, source_target_pairs={{0,3},{1,0},{2,1},{3,2},{4,7},{5,4},{6,5},{7,6},{8,11},{9,8},{10,9... | collective-permute-start | bytes 1572872 | tf_op jit(solution)/shard_map/ppermute | solution.py:282
  60.7 44.1 %all-to-all-start.1 = ((bf16[32,96,256]{2,1,0:T(8,128)(2,1)}), bf16[32,96,256]{2,1,0:T(8,128)(2,1)}, u32[]{:S(2)}, u32[]{:S(2)}) async-start(bf16[32,96,256]{2,1,0:T(8,128)(2,1)} %bitcast.24), calls=%async_computation.1 | async-start | bytes 3145728 | tf_op jit(solution)/shard_map/all_to_all | solution.py:320
  71.4 9.4 %collective-permute-start = (bf16[512,256]{1,0:T(8,128)(2,1)S(1)}, bf16[512,256]{1,0:T(8,128)(2,1)}, u32[]{:S(2)}, u32[]{:S(2)}) collective-permute-start(bf16[512,256]{1,0:T(8,128)(2,1)S(1)} %get-tuple-element.24.up_ref), channel_id=1, source_target_pairs={{0,1},{1,2},{2,3},{3,0},{4,5},{5,6},{6,7},{7,4},{8,9},{9,10},{10,1... | collective-permute-start | bytes 786440 | tf_op jit(solution)/shard_map/ppermute | solution.py:282
  72.9 9.6 %collective-permute-start.3 = (bf16[512,256]{1,0:T(8,128)(2,1)}, bf16[512,256]{1,0:T(8,128)(2,1)}, u32[]{:S(2)}, u32[]{:S(2)}) collective-permute-start(bf16[512,256]{1,0:T(8,128)(2,1)} %get-tuple-element.25.low_ref), channel_id=1, source_target_pairs={{0,3},{1,0},{2,1},{3,2},{4,7},{5,4},{6,5},{7,6},{8,11},{9,8},{10,9... | collective-permute-start | bytes 786440 | tf_op jit(solution)/shard_map/ppermute | solution.py:282
  73.4 12.9 %collective-permute-start.1 = (bf16[512,256]{1,0:T(8,128)(2,1)}, bf16[512,256]{1,0:T(8,128)(2,1)}, u32[]{:S(2)}, u32[]{:S(2)}) collective-permute-start(bf16[512,256]{1,0:T(8,128)(2,1)} %get-tuple-element.25.low_ref), channel_id=1, source_target_pairs={{0,1},{1,2},{2,3},{3,0},{4,5},{5,6},{6,7},{7,4},{8,9},{9,10},{10,1... | collective-permute-start | bytes 786440 | tf_op jit(solution)/shard_map/ppermute | solution.py:282
  75.0 13.2 %collective-permute-start.2 = (bf16[512,256]{1,0:T(8,128)(2,1)S(1)}, bf16[512,256]{1,0:T(8,128)(2,1)}, u32[]{:S(2)}, u32[]{:S(2)}) collective-permute-start(bf16[512,256]{1,0:T(8,128)(2,1)S(1)} %get-tuple-element.24.up_ref), channel_id=1, source_target_pairs={{0,3},{1,0},{2,1},{3,2},{4,7},{5,4},{6,5},{7,6},{8,11},{9,8},{10,9... | collective-permute-start | bytes 786440 | tf_op jit(solution)/shard_map/ppermute | solution.py:282
  80.7 9.6 %collective-permute-start.4 = (bf16[512,256]{1,0:T(8,128)(2,1)}, bf16[512,256]{1,0:T(8,128)(2,1)}, u32[]{:S(2)}, u32[]{:S(2)}) collective-permute-start(bf16[512,256]{1,0:T(8,128)(2,1)} %collective-permute-done.lu_ref), channel_id=1, source_target_pairs={{0,1},{1,2},{2,3},{3,0},{4,5},{5,6},{6,7},{7,4},{8,9},{9,10},{10,1... | collective-permute-start | bytes 786440 | tf_op jit(solution)/shard_map/ppermute | solution.py:282
  82.5 9.4 %collective-permute-start.5 = (bf16[512,256]{1,0:T(8,128)(2,1)}, bf16[512,256]{1,0:T(8,128)(2,1)}, u32[]{:S(2)}, u32[]{:S(2)}) collective-permute-start(bf16[512,256]{1,0:T(8,128)(2,1)} %collective-permute-done.3.rl_ref), channel_id=1, source_target_pairs={{0,3},{1,0},{2,1},{3,2},{4,7},{5,4},{6,5},{7,6},{8,11},{9,8},{10,9... | collective-permute-start | bytes 786440 | tf_op jit(solution)/shard_map/ppermute | solution.py:282
  104.8 43.8 %all-to-all-start.2 = ((bf16[32,96,256]{2,1,0:T(8,128)(2,1)}), bf16[32,96,256]{2,1,0:T(8,128)(2,1)}, u32[]{:S(2)}, u32[]{:S(2)}) async-start(bf16[32,96,256]{2,1,0:T(8,128)(2,1)} %bitcast.23), calls=%async_computation.2 | async-start | bytes 3145728 | tf_op jit(solution)/shard_map/all_to_all | solution.py:320
  115.5 9.3 %collective-permute-start.11 = (bf16[512,256]{1,0:T(8,128)(2,1)S(1)}, bf16[512,256]{1,0:T(8,128)(2,1)S(1)}, u32[]{:S(2)}, u32[]{:S(2)}) collective-permute-start(bf16[512,256]{1,0:T(8,128)(2,1)S(1)} %get-tuple-element.33.up_ref), channel_id=1, source_target_pairs={{0,1},{1,2},{2,3},{3,0},{4,5},{5,6},{6,7},{7,4},{8,9},{9,10},{10,1... | collective-permute-start | bytes 786440 | tf_op jit(solution)/shard_map/ppermute | solution.py:282
  117.6 12.8 %collective-permute-start.12 = (bf16[512,256]{1,0:T(8,128)(2,1)S(1)}, bf16[512,256]{1,0:T(8,128)(2,1)S(1)}, u32[]{:S(2)}, u32[]{:S(2)}) collective-permute-start(bf16[512,256]{1,0:T(8,128)(2,1)S(1)} %get-tuple-element.34.low_ref), channel_id=1, source_target_pairs={{0,1},{1,2},{2,3},{3,0},{4,5},{5,6},{6,7},{7,4},{8,9},{9,10},{10,1... | collective-permute-start | bytes 786440 | tf_op jit(solution)/shard_map/ppermute | solution.py:282
  119.2 12.7 %collective-permute-start.13 = (bf16[512,256]{1,0:T(8,128)(2,1)S(1)}, bf16[512,256]{1,0:T(8,128)(2,1)S(1)}, u32[]{:S(2)}, u32[]{:S(2)}) collective-permute-start(bf16[512,256]{1,0:T(8,128)(2,1)S(1)} %get-tuple-element.33.up_ref), channel_id=1, source_target_pairs={{0,3},{1,0},{2,1},{3,2},{4,7},{5,4},{6,5},{7,6},{8,11},{9,8},{10,9... | collective-permute-start | bytes 786440 | tf_op jit(solution)/shard_map/ppermute | solution.py:282
  156.5 12.5 %collective-permute-start.17 = (bf16[512,256]{1,0:T(8,128)(2,1)}, bf16[512,256]{1,0:T(8,128)(2,1)S(1)}, u32[]{:S(2)}, u32[]{:S(2)}) collective-permute-start(bf16[512,256]{1,0:T(8,128)(2,1)} %get-tuple-element.41.up_ref), channel_id=1, source_target_pairs={{0,1},{1,2},{2,3},{3,0},{4,5},{5,6},{6,7},{7,4},{8,9},{9,10},{10,1... | collective-permute-start | bytes 786440 | tf_op jit(solution)/shard_map/ppermute | solution.py:282
  158.2 12.3 %collective-permute-start.20 = (bf16[512,256]{1,0:T(8,128)(2,1)}, bf16[512,256]{1,0:T(8,128)(2,1)S(1)}, u32[]{:S(2)}, u32[]{:S(2)}) collective-permute-start(bf16[512,256]{1,0:T(8,128)(2,1)} %get-tuple-element.42.low_ref), channel_id=1, source_target_pairs={{0,3},{1,0},{2,1},{3,2},{4,7},{5,4},{6,5},{7,6},{8,11},{9,8},{10,9... | collective-permute-start | bytes 786440 | tf_op jit(solution)/shard_map/ppermute | solution.py:282
  159.4 14.8 %all-to-all-start.3 = ((bf16[16,32,256]{2,1,0:T(8,128)(2,1)}), bf16[16,32,256]{2,1,0:T(8,128)(2,1)S(1)}, u32[]{:S(2)}, u32[]{:S(2)}) async-start(bf16[16,32,256]{2,1,0:T(8,128)(2,1)} %bitcast.16), calls=%async_computation.3 | async-start | bytes 524288 | tf_op jit(solution)/shard_map/all_to_all | solution.py:302
  167.0 11.3 %collective-permute-start.18 = (bf16[512,256]{1,0:T(8,128)(2,1)}, bf16[512,256]{1,0:T(8,128)(2,1)S(1)}, u32[]{:S(2)}, u32[]{:S(2)}) collective-permute-start(bf16[512,256]{1,0:T(8,128)(2,1)} %get-tuple-element.42.low_ref), channel_id=1, source_target_pairs={{0,1},{1,2},{2,3},{3,0},{4,5},{5,6},{6,7},{7,4},{8,9},{9,10},{10,1... | collective-permute-start | bytes 786440 | tf_op jit(solution)/shard_map/ppermute | solution.py:282
  168.5 11.0 %collective-permute-start.19 = (bf16[512,256]{1,0:T(8,128)(2,1)}, bf16[512,256]{1,0:T(8,128)(2,1)S(1)}, u32[]{:S(2)}, u32[]{:S(2)}) collective-permute-start(bf16[512,256]{1,0:T(8,128)(2,1)} %get-tuple-element.41.up_ref), channel_id=1, source_target_pairs={{0,3},{1,0},{2,1},{3,2},{4,7},{5,4},{6,5},{7,6},{8,11},{9,8},{10,9... | collective-permute-start | bytes 786440 | tf_op jit(solution)/shard_map/ppermute | solution.py:282
  169.0 13.5 %collective-permute-start.21 = (bf16[512,256]{1,0:T(8,128)(2,1)S(1)}, bf16[512,256]{1,0:T(8,128)(2,1)S(1)}, u32[]{:S(2)}, u32[]{:S(2)}) collective-permute-start(bf16[512,256]{1,0:T(8,128)(2,1)S(1)} %collective-permute-done.17.lu_ref), channel_id=1, source_target_pairs={{0,1},{1,2},{2,3},{3,0},{4,5},{5,6},{6,7},{7,4},{8,9},{9,10},{10,1... | collective-permute-start | bytes 786440 | tf_op jit(solution)/shard_map/ppermute | solution.py:282
  170.5 13.4 %collective-permute-start.22 = (bf16[512,256]{1,0:T(8,128)(2,1)S(1)}, bf16[512,256]{1,0:T(8,128)(2,1)S(1)}, u32[]{:S(2)}, u32[]{:S(2)}) collective-permute-start(bf16[512,256]{1,0:T(8,128)(2,1)S(1)} %collective-permute-done.20.rl_ref), channel_id=1, source_target_pairs={{0,3},{1,0},{2,1},{3,2},{4,7},{5,4},{6,5},{7,6},{8,11},{9,8},{10,9... | collective-permute-start | bytes 786440 | tf_op jit(solution)/shard_map/ppermute | solution.py:282
  174.9 12.4 %all-to-all-start.4 = ((f32[8,16,256]{2,1,0:T(8,128)}), f32[8,16,256]{2,1,0:T(8,128)S(1)}, u32[]{:S(2)}, u32[]{:S(2)}) async-start(f32[8,16,256]{2,1,0:T(8,128)} %convert_reduce_fusion), calls=%async_computation.4 | async-start | bytes 262144 | tf_op jit(solution)/shard_map/all_to_all | solution.py:304
  (33 other events, 172.4 us)
